TPU v7x, 128 devices: a whole 4x4x4 slice. The times are simulated.
128 devices in a mesh: dp: 4 (over y), seq: 32 (over z, x, core).
Axes of the slice: x: 4, y: 4, z: 4, core: 2. Of those that a mesh axis runs over, the one named last changes fastest.
Arguments:
- tile_rows: bfloat16 [4, 65536, 768], P('dp', 'seq'), may hold values from -6 to 6
- block_dest: int32 [4, 512], P('dp', 'seq'), may hold values from 0 to 31, as said below
- norm_gain: float32 [768], replicated, may hold values from 0.25 to 1.75
- qkv_weight: bfloat16 [768, 2304], replicated, may hold values from -1 to 1
- out_weight: bfloat16 [768, 768], replicated, may hold values from -0.21875 to 0.21875
- cotangent: bfloat16 [4, 65536, 768], P('dp', 'seq'), may hold values from -0.0625 to 0.0625
Outputs:
- encoded: bfloat16 [4, 65536, 768], P('dp', 'seq')
- out_weight_grad: float32 [768, 768], P('seq')
Inputs may be any that keep to these rules, and one draw needn't show every extreme that they name: `block_dest`: in each slide every destination shard is named exactly 16 times, and the 16 blocks of one source shard name 16 different destinations, so one destination at most 1 times.
All inputs are finite; a program needn't handle non-finite values.
Results may differ from a plain program's by a relative error of at most 0.022.
The roundings to bfloat16 on the way count: a program that leaves them out, or rounds other values in their place, can miss the bound.
Values may be sent and summed in bfloat16 or wider, within the bound.
A program may use at most 192 MiB of HBM per device.

v0:
```python
import jax
import jax.numpy as jnp
import numpy as np
from jax import lax
from jax.sharding import PartitionSpec as P

HEADS = 12
HEAD_DIM = 64
BLK = 128
CAP = 1
SEG = 512
RATE = 16


score_scale = 0.125
norm_eps = 1e-06


def normalize(values, norm_gain):
    values = values.astype(jnp.float32)
    center = values - jnp.mean(values, axis=-1, keepdims=True)
    spread = jnp.mean(center * center, axis=-1, keepdims=True)
    return (center * lax.rsqrt(spread + norm_eps) * norm_gain).astype(jnp.bfloat16)


def local_segment(queries, keys_seg, values_seg):
    scores = (
        jnp.einsum("sqhd,skhd->shqk", queries, keys_seg, preferred_element_type=jnp.float32)
        * score_scale
    )
    peak = jnp.max(scores, axis=-1)
    weights = jnp.exp(scores - peak[..., None])
    total = jnp.sum(weights, axis=-1)
    mixed = jnp.einsum(
        "shqk,skhd->sqhd",
        weights.astype(jnp.bfloat16),
        values_seg,
        preferred_element_type=jnp.float32,
    )
    total_t = jnp.swapaxes(total, 1, 2)
    return (mixed / total_t[..., None], jnp.swapaxes(peak, 1, 2) + jnp.log(total_t))


def place_blocks(received, local_blocks):
    got_blocks, got_counts = received
    shards = got_blocks.shape[1]
    slot_total = shards * CAP
    send_ids = jnp.arange(slot_total, dtype=jnp.int32)
    slot_ids = jnp.arange(local_blocks, dtype=jnp.int32)
    counts = got_counts[:, :, 0].astype(jnp.int32)
    starts = jnp.cumsum(counts, axis=1) - counts
    source_of = send_ids // CAP
    within = send_ids % CAP
    target = starts[:, source_of] + within[None, :]
    live = within[None, :] < counts[:, source_of]
    taking = jnp.logical_and(
        target[:, None, :] == slot_ids[None, :, None], live[:, None, :]
    ).astype(jnp.bfloat16)
    return jnp.einsum(
        "skp,spx->skx", taking, got_blocks, preferred_element_type=jnp.float32
    ).astype(jnp.bfloat16)


def body(tile_rows, block_dest, norm_gain, qkv_weight, out_weight, cotangent):
    shards = lax.axis_size("seq")
    slides, rows, width = tile_rows.shape
    local_blocks = rows // BLK
    far_rows = rows // RATE
    blocks = tile_rows.reshape(slides, local_blocks, BLK * width)
    slot_ids = jnp.arange(local_blocks)
    same_dest = block_dest[:, :, None] == block_dest[:, None, :]
    before = slot_ids[None, None, :] < slot_ids[None, :, None]
    rank = jnp.sum(jnp.logical_and(same_dest, before), axis=-1)
    position = block_dest * CAP + rank
    send_ids = jnp.arange(shards * CAP, dtype=jnp.int32)
    placing = (position[:, None, :] == send_ids[None, :, None]).astype(jnp.bfloat16)
    send_blocks = jnp.einsum(
        "spj,sjx->spx", placing, blocks, preferred_element_type=jnp.float32
    ).astype(jnp.bfloat16)
    shard_ids = jnp.arange(shards, dtype=jnp.int32)
    send_counts = jnp.sum(
        (block_dest[:, :, None] == shard_ids[None, None, :]).astype(jnp.float32), axis=1
    )
    send_counts = send_counts[:, :, None].astype(jnp.bfloat16)
    got_blocks, got_counts = (
        lax.all_to_all(send_blocks, "seq", split_axis=1, concat_axis=1, tiled=True),
        lax.all_to_all(send_counts, "seq", split_axis=1, concat_axis=1, tiled=True),
    )
    placed = place_blocks((got_blocks, got_counts), local_blocks)
    inputs = placed.reshape(slides, rows, width)
    normed = normalize(inputs, norm_gain)
    qkv = jnp.einsum("srd,de->sre", normed, qkv_weight, preferred_element_type=jnp.float32).astype(
        jnp.bfloat16
    )
    segs = rows // SEG
    qkv_segs = qkv.reshape(slides, segs, SEG, 3 * width)

    def segment_step(index, carry):
        near_acc, lse_acc = carry
        piece = lax.dynamic_index_in_dim(qkv_segs, index, 1, keepdims=False)
        seg_q = piece[:, :, :width].reshape(slides, SEG, HEADS, HEAD_DIM)
        seg_k = piece[:, :, width : 2 * width].reshape(slides, SEG, HEADS, HEAD_DIM)
        seg_v = piece[:, :, 2 * width :].reshape(slides, SEG, HEADS, HEAD_DIM)
        seg_out, seg_lse = local_segment(seg_q, seg_k, seg_v)
        near_acc = lax.dynamic_update_slice_in_dim(
            near_acc, seg_out.reshape(slides, SEG, width), index * SEG, 1
        )
        lse_acc = lax.dynamic_update_slice_in_dim(lse_acc, seg_lse, index * SEG, 1)
        return (near_acc, lse_acc)

    near_flat, near_lse = lax.fori_loop(
        0,
        segs,
        segment_step,
        (
            jnp.zeros((slides, rows, width), jnp.float32),
            jnp.zeros((slides, rows, HEADS), jnp.float32),
        ),
    )
    far_inputs = normed.reshape(slides, far_rows, RATE, width)[:, :, :HEADS, :]
    head_weight = jnp.transpose(
        qkv_weight.reshape(width, 3, HEADS, HEAD_DIM), (2, 0, 1, 3)
    ).reshape(HEADS, width, 3 * HEAD_DIM)
    far_qkv = jnp.einsum(
        "sfhd,hde->shfe", far_inputs, head_weight, preferred_element_type=jnp.float32
    ).astype(jnp.bfloat16)
    query_far = far_qkv[..., :HEAD_DIM]
    kv_far = far_qkv[..., HEAD_DIM:]
    piece = lax.all_gather(kv_far, "seq", axis=2, tiled=True)
    peak = jnp.full((slides, HEADS, far_rows), -1e30, jnp.float32)
    key_piece = piece[..., :HEAD_DIM]
    value_piece = piece[..., HEAD_DIM:]
    scores = (
        jnp.einsum("shqd,shnd->shqn", query_far, key_piece, preferred_element_type=jnp.float32)
        * score_scale
    )
    new_peak = jnp.maximum(peak, jnp.max(scores, axis=-1))
    weights = jnp.exp(scores - new_peak[..., None])
    total = jnp.sum(weights, axis=-1)
    accum = jnp.einsum(
        "shqn,shnd->shqd",
        weights.astype(jnp.bfloat16),
        value_piece,
        preferred_element_type=jnp.float32,
    )
    peak, total, accum = (new_peak, total, accum)
    far_out = accum / total[..., None]
    far_lse = peak + jnp.log(total)
    chosen = (np.arange(RATE)[:, None] == (np.arange(HEADS) % RATE)[None, :]).astype(np.float32)
    chosen_table = jnp.asarray(chosen)
    near_rows = near_flat.reshape(slides, far_rows, RATE, HEADS, HEAD_DIM)
    lse_rows = near_lse.reshape(slides, far_rows, RATE, HEADS)
    near_sel = jnp.einsum(
        "sfrhd,rh->sfhd", near_rows, chosen_table, precision=lax.Precision.HIGHEST
    )
    lse_sel = jnp.einsum("sfrh,rh->sfh", lse_rows, chosen_table, precision=lax.Precision.HIGHEST)
    far_t = jnp.swapaxes(far_out, 1, 2)
    far_lse_t = jnp.swapaxes(far_lse, 1, 2)
    top = jnp.maximum(lse_sel, far_lse_t)
    near_share = jnp.exp(lse_sel - top)
    far_share = jnp.exp(far_lse_t - top)
    mixed = (near_share[..., None] * near_sel + far_share[..., None] * far_t) / (
        near_share + far_share
    )[..., None]
    chosen_mask = jnp.asarray(chosen > 0.5)[None, None, :, :, None]
    merged = jnp.where(chosen_mask, mixed[:, :, None, :, :], near_rows)
    attn = merged.reshape(slides, rows, width).astype(jnp.bfloat16)
    projected = jnp.einsum("srd,de->sre", attn, out_weight, preferred_element_type=jnp.float32)
    encoded = (inputs.astype(jnp.float32) + projected).astype(jnp.bfloat16)
    grad_local = jnp.einsum("srd,sre->de", attn, cotangent, preferred_element_type=jnp.float32)
    grad_slides = lax.psum(grad_local.astype(jnp.bfloat16), "dp")
    grad_mine = lax.psum_scatter(grad_slides, "seq", scatter_dimension=0, tiled=True).astype(
        jnp.float32
    )
    return (encoded, grad_mine)


def solution(mesh):
    return jax.shard_map(
        body,
        mesh=mesh,
        in_specs=(P("dp", "seq", None), P("dp", "seq"), P(), P(), P(), P("dp", "seq", None)),
        out_specs=(P("dp", "seq", None), P("seq", None)),
        check_vma=False,
    )
```

profile of v0, /device:TPU:0, one launch (start us, length us, event | category | flops | bytes accessed | tf_op | source)
XLA Modules:
  0.0 580.1 jit_solution(17526144849962561025)
XLA Ops:
  8.8 8.2 %all-to-all-start = ((bf16[1,32,1]{2,0,1:T(2,128)(2,1)}), bf16[1,32,1]{2,0,1:T(2,128)(2,1)S(1)}, u32[]{:S(2)}, u32[]{:S(2)}) async-start(bf16[1,32,1]{2,0,1:T(2,128)(2,1)} %copy.58), calls=%async_computation | async-start | bytes 32768 | tf_op jit(solution)/shard_map/all_to_all | solution.py:87
  26.3 31.0 %copy.120 = bf16[1,32,98304]{2,0,1:T(2,128)(2,1)} copy(bf16[1,32,98304]{2,1,0:T(8,128)(2,1)S(1)} %fusion.10) | data formatting | bytes 12582912 | tf_op jit(solution)/shard_map/convert_element_type | solution.py:79
  57.8 39.4 %reduce.21 = bf16[32,98304]{1,0:T(8,128)(2,1)} reduce(bf16[32,1,98304]{2,1,0:T(2,128)(2,1)} %bitcast.197, bf16[]{:T(256)} %broadcast.342), dimensions={1}, to_apply=%bitcast.165.reduce_sub_computation | reduce | bytes 12582914
  97.1 8.8 %reshape.623 = bf16[32,2,49152]{2,1,0:T(2,128)(2,1)} reshape(bf16[32,98304]{1,0:T(8,128)(2,1)} %reduce.21) | data formatting | bytes 12582912
  105.9 7.5 %all-to-all-start.1 = ((bf16[32,2,49152]{2,1,0:T(2,128)(2,1)}), bf16[32,2,49152]{2,1,0:T(2,128)(2,1)}, u32[]{:S(2)}, u32[]{:S(2)}) async-start(bf16[32,2,49152]{2,1,0:T(2,128)(2,1)} %reshape.623), calls=%async_computation.1 | async-start | bytes 12582912 | tf_op jit(solution)/shard_map/all_to_all | solution.py:86
  113.7 5.8 copy.64
  126.0 65.3 %all-to-all-done.1 = bf16[32,2,49152]{2,1,0:T(2,128)(2,1)} async-done(((bf16[32,2,49152]{2,1,0:T(2,128)(2,1)}), bf16[32,2,49152]{2,1,0:T(2,128)(2,1)}, u32[]{:S(2)}, u32[]{:S(2)}) %all-to-all-start.1) | async-done | bytes 6291488 | tf_op jit(solution)/shard_map/all_to_all | solution.py:86
  191.3 21.6 %reshape.624 = bf16[32,1,98304]{2,1,0:T(2,128)(2,1)} reshape(bf16[32,2,49152]{2,1,0:T(2,128)(2,1)} %all-to-all-done.1) | data formatting | bytes 12582912
  212.9 14.0 %fusion.11 = f32[16,98304]{1,0:T(8,128)} fusion(bf16[1,32,98304]{2,0,1:T(2,128)(2,1)} %bitcast.199, s32[32]{0:T(128)S(1)} %gather_fusion, pred[32]{0:T(512)(128)(4,1)S(1)} %broadcast_compare_fusion), kind=kOutput, calls=%fused_computation.19 | convolution fusion | flops 103810048 | bytes 12583072 | tf_op jit(solution)/shard_map/skp,spx->skx/dot_general | solution.py:59
  244.1 7.1 %fusion.43 = bf16[1,12,128,192]{2,3,1,0:T(8,128)(2,1)S(1)} fusion(bf16[12,768,192]{1,2,0:T(8,128)(2,1)} %bitcast.204, f32[1,128,12,768]{3,2,1,0:T(8,128)} %bitcast.203, f32[768]{0:T(1024)S(1)} %copy-done.6, f32[128,12]{0,1:T(8,128)S(1)} %copy.117, f32[128,12]{0,1:T(8,128)S(1)} %copy.118), kind=kOutput, calls=%fused_computation.56 | convolution fusion | flops 457998336 | bytes 8862720 | tf_op jit(solution)/shard_map/sfhd,hde->shfe/dot_general | solution.py:124
  257.0 18.3 %broadcast_in_dim.29 = pred[1,2048,768]{2,1,0:T(8,128)(4,1)} reshape(pred[128,16,12,64]{3,2,1,0:T(8,128)(4,1)} %broadcast_in_dim.28) | data formatting | bytes 3145728 | tf_op jit(solution)/shard_map/jit(_where)/broadcast_in_dim | solution.py:166
  280.3 13.1 %convolution_convert_fusion.2 = bf16[2048,2304]{1,0:T(8,128)(2,1)} fusion(bf16[768,2304]{1,0:T(8,128)(2,1)} %param.13, f32[2048,768]{1,0:T(8,128)} %reshape.589, f32[768]{0:T(1024)S(1)} %copy-done.6, f32[2048]{0:T(1024)S(1)} %add_rsqrt_fusion, f32[2048]{0:T(1024)S(1)} %broadcast_multiply_fusion), kind=kOutput, calls=%fused_computation.28 | convolution fusion | flops 7258767360 | bytes 19287040 | tf_op jit(solution)/shard_map/srd,de->sre/dot_general | solution.py:92
  296.4 89.7 %while.15 = (s32[]{:T(128)}, f32[1,2048,768]{2,1,0:T(8,128)}, f32[1,2048,12]{1,2,0:T(8,128)S(1)}, bf16[1,4,512,2304]{3,2,1,0:T(8,128)(2,1)}, s32[]{:T(128)}, /*index=5*/s32[]{:T(128)}, s32[]{:T(128)}, s32[]{:T(128)}) while((s32[]{:T(128)}, f32[1,2048,768]{2,1,0:T(8,128)}, f32[1,2048,12]{1,2,0:T(8,128)S(1)}, ...), condition=%wide.region_8.9_spmd, body=%wide.region_5.8_spmd.sunk | while | flops 830859264 | bytes 62349460 | solution.py:111
  387.3 12.1 %reshape.584 = f32[128,16,12,64]{3,2,1,0:T(8,128)} reshape(f32[1,2048,768]{2,1,0:T(8,128)} %get-tuple-element.83) | data formatting | bytes 12582912 | tf_op jit(solution)/shard_map/reshape.55
  399.4 9.5 %multiply_reduce_fusion.2 = f32[12,128,64]{2,0,1:T(8,128)} fusion(f32[128,16,12,64]{3,2,1,0:T(8,128)} %reshape.584, f32[12,16]{0,1:T(8,128)S(1)} %copy-done.3), kind=kLoop, calls=%fused_computation.24 | loop fusion | flops 3047424 | bytes 6685440
  412.9 14.7 %multiply_reduce_fusion.1 = (f32[12,128]{1,0:T(8,128)S(1)}, f32[12,128,4096]{2,1,0:T(8,128)}) fusion(bf16[1,12,4096,128]{2,3,1,0:T(8,128)(2,1)} %all-gather.2.cloned.1.call-done, bf16[1,12,128,192]{2,3,1,0:T(8,128)(2,1)} %copy-done.2), kind=kOutput, calls=%fused_computation.21 | convolution fusion | flops 817887744 | bytes 31660032 | tf_op jit(solution)/shard_map/shqd,shnd->shqn/dot_general | solution.py:134
  427.6 10.8 %fusion.13 = f32[12,128]{1,0:T(8,128)S(1)} fusion(f32[12,128,4096]{2,1,0:T(8,128)} %get-tuple-element.125, f32[12,128]{1,0:T(8,128)S(1)} %broadcast_maximum_fusion), kind=kLoop, calls=%fused_computation.23 | loop fusion | flops 18872832 | bytes 25178112 | tf_op jit(solution)/shard_map/reduce_sum | solution.py:139
  438.4 13.4 %fusion.61 = bf16[128,12,64]{0,2,1:T(8,128)(2,1)} fusion(bf16[1,12,4096,128]{2,3,1,0:T(8,128)(2,1)} %all-gather.2.cloned.1.call-done, f32[12,128,4096]{2,1,0:T(8,128)} %get-tuple-element.125, f32[12,128]{1,0:T(8,128)S(1)} %broadcast_maximum_fusion, f32[12,128,64]{1,2,0:T(8,128)S(1)} %copy.78, f32[128,12]{0,1:T(8,128)S(1)} %get-tuple-element.122, ...), kind=kOutput, calls=%fused_computation.62 | convolution fusion | flops 824770560 | bytes 32077824 | tf_op jit(solution)/shard_map/shqn,shnd->shqd/dot_general | solution.py:140
  453.9 5.3 broadcast_in_dim.34
  459.3 11.1 %broadcast_in_dim.35 = bf16[1,2048,768]{2,1,0:T(8,128)(2,1)} reshape(bf16[128,16,12,64]{3,2,1,0:T(8,128)(2,1)} %broadcast_in_dim.34) | data formatting | bytes 6291456 | tf_op jit(solution)/shard_map/jit(_where)/broadcast_in_dim | solution.py:166
  470.4 5.1 fusion.24
  481.0 8.4 %fusion.30 = bf16[1,2048,768]{2,1,0:T(8,128)(2,1)} fusion(f32[2048,768]{1,0:T(8,128)} %reshape.589, bf16[2048,768]{1,0:T(8,128)(2,1)} %copy-done.1, bf16[768,768]{1,0:T(8,128)(2,1)} %param.14), kind=kOutput, calls=%fused_computation.48 | convolution fusion | flops 2419064832 | bytes 13762560 | tf_op jit(solution)/shard_map/srd,de->sre/dot_general | solution.py:168
  489.4 65.0 %reduce-scatter.2.cloned.1.call-done = bf16[24,768]{1,0:T(8,128)(2,1)} async-done(((bf16[768,768]{1,0:T(8,128)(2,1)}), bf16[24,768]{1,0:T(8,128)(2,1)}) %reduce-scatter.2.cloned.1.call-update) | async-done | bytes 36880 | tf_op jit(solution)/shard_map/reduce_scatter | solution.py:172
  554.3 17.8 %psum.8 = bf16[24,768]{1,0:T(8,128)(2,1)S(1)} all-reduce(bf16[24,768]{1,0:T(8,128)(2,1)} %reduce-scatter.2.cloned.1.call-done), channel_id=1, replica_groups=mesh['dp'=4,'seq'=32] {'dp'}, use_global_device_ids=true, to_apply=%region_11.12 | all-reduce | flops 18432 | bytes 73728 | tf_op jit(solution)/shard_map/psum | solution.py:171
  (95 shorter events, 152.0 us)
Async XLA Ops:
  7.2 470.0 %copy-start = (bf16[1,2048,768]{2,1,0:T(8,128)(2,1)S(1)}, bf16[1,2048,768]{2,1,0:T(8,128)(2,1)}, u32[]{:S(2)}) copy-start(bf16[1,2048,768]{2,1,0:T(8,128)(2,1)} %param.15) | copy-start | bytes 9437188
  8.8 97.1 %all-to-all-start = ((bf16[1,32,1]{2,0,1:T(2,128)(2,1)}), bf16[1,32,1]{2,0,1:T(2,128)(2,1)S(1)}, u32[]{:S(2)}, u32[]{:S(2)}) async-start(bf16[1,32,1]{2,0,1:T(2,128)(2,1)} %copy.58), calls=%async_computation | async-start | bytes 32768 | tf_op jit(solution)/shard_map/all_to_all | solution.py:87
  105.9 85.4 %all-to-all-start.1 = ((bf16[32,2,49152]{2,1,0:T(2,128)(2,1)}), bf16[32,2,49152]{2,1,0:T(2,128)(2,1)}, u32[]{:S(2)}, u32[]{:S(2)}) async-start(bf16[32,2,49152]{2,1,0:T(2,128)(2,1)} %reshape.623), calls=%async_computation.1 | async-start | bytes 12582912 | tf_op jit(solution)/shard_map/all_to_all | solution.py:86
  113.4 299.5 %all-gather.2.cloned.1.call-start = ((), (), s32[]{:S(2)}) async-start(), calls=%async_computation.3 | async-start | bytes 12976128 | tf_op jit(solution)/shard_map/all_gather | solution.py:129
  238.8 5.3 copy-start.6
  243.8 9.0 %copy-start.5 = (pred[16,12]{1,0:T(8,128)(4,1)S(1)}, pred[16,12]{1,0:T(8,128)(4,1)}, u32[]{:S(2)}) copy-start(pred[16,12]{1,0:T(8,128)(4,1)} %constant.109.clone) | copy-start | bytes 580
  251.1 0.8 copy-start.2
  252.8 301.5 %reduce-scatter.2.cloned.1.call-start = ((), (), s32[]{:S(2)}) async-start(), calls=%async_computation.4 | async-start | bytes 1216512 | tf_op jit(solution)/shard_map/reduce_scatter | solution.py:172
  387.3 12.1 %copy-start.3 = (f32[12,16]{0,1:T(8,128)S(1)}, f32[12,16]{0,1:T(8,128)}, u32[]{:S(2)}) copy-start(f32[12,16]{0,1:T(8,128)} %constant.116) | copy-start | bytes 2308
  399.4 11.1 %copy-start.4 = (f32[16,12,1]{0,2,1:T(1,128)S(1)}, f32[16,12,1]{0,2,1:T(1,128)}, u32[]{:S(2)}) copy-start(f32[16,12,1]{0,2,1:T(1,128)} %constant.115) | copy-start | bytes 2308
  475.5 1.7 copy-start.1
Sparse Core Ops, SparseCore 0:
  252.9 67.2 all-gather.1
  481.1 73.2 reduce-scatter.1
where the time goes:
time: 590 us; the launch traced here: 580 us
  local copies, waits for them, and re-layouts  216 us (37%)
  waiting for transfers between devices  130 us (22%)
  matrix products  101 us (17%)
  other arithmetic  84 us (14%)
  blocking collectives  17.8 us (3%)
  starting transfers between devices  16.1 us (3%)
  between operations  14.6 us (2%)
    all_to_all x1, waiting for transfers between devices, body(): lax.all_to_all(send_blocks, 'seq', split_axis=1, concat_axis=1, tiled=True)  65.3 us
    reduce_scatter x1, waiting for transfers between devices, body(): lax.psum_scatter(grad_slides, 'seq', scatter_dimension=0, tiled=True)  65 us
    unnamed x2, other arithmetic  48.9 us
    broadcast_in_dim x5, local copies, waits for them, and re-layouts, body(): merged = jnp.where(chosen_mask, mixed[:, :, None, :, :], near_rows)  41 us
    unnamed x20, local copies, waits for them, and re-layouts  39.3 us
    convert_element_type x1, local copies, waits for them, and re-layouts, body(): send_blocks = jnp.einsum('spj,sjx->spx', placing, blocks, preferred_eleme...  31 us
    dynamic_slice x8, local copies, waits for them, and re-layouts, segment_step(): piece = lax.dynamic_index_in_dim(qkv_segs, index, 1, keepdims=False)  30.3 us
    dynamic_update_slice x8, local copies, waits for them, and re-layouts, segment_step(): lax.dynamic_update_slice_in_dim(near_acc, seg_out.reshape(slides, SEG, wi...  23 us
  transfers between devices with their start and end apart: 4, of which 2 were waited for; matrix products, arithmetic and copies ran while one was open for 46% of the time, Pallas kernels for 0%

commit v1 on v0

v1 whole, which is shorter than its diff:
```python
import functools

import jax
import jax.numpy as jnp
from jax import lax
from jax.experimental import pallas as pl
from jax.experimental.pallas import tpu as pltpu
from jax.sharding import PartitionSpec as P

WIDTH = 768
HEADS = 12
HEAD_DIM = 64
BLK = 128
SEG = 512
RATE = 16
ROWS = 2048
SHARDS = 32
SLIDES = 4
SEGS = ROWS // SEG
STRIDE = 32
PAIRS = HEADS // 2
GROUPS = WIDTH // 128
FAR_OWNERS = 2 * HEADS
MESH = pl.DeviceIdType.MESH

score_scale = 0.125
norm_eps = 1e-06


def lanes(group):
    return slice(128 * group, 128 * group + 128)


def row_class(shard):
    return RATE * lax.rem(shard, 2) + lax.div(shard, 2)


def peer(me, step):
    z, x, c = lax.div(me, 8), lax.rem(lax.div(me, 2), 4), lax.rem(me, 2)
    dz = lax.rem(step, 4)
    dx = lax.rem(step + lax.div(step, 8), 4)
    dc = lax.rem(lax.div(step, 4), 2)
    return lax.rem(z + dz, 4) * 8 + lax.rem(x + dx, 4) * 2 + lax.rem(c + dc, 2)


def normalize(values, gain):
    center = values - jnp.mean(values, axis=-1, keepdims=True)
    spread = jnp.mean(center * center, axis=-1, keepdims=True)
    return (center * lax.rsqrt(spread + norm_eps) * gain).astype(jnp.bfloat16)


def dot(a, b):
    return jnp.dot(a, b, preferred_element_type=jnp.float32)


def dot_t(a, b):
    return lax.dot_general(a, b, (((1,), (1,)), ((), ())), preferred_element_type=jnp.float32)


def iota(shape, dim):
    return lax.broadcasted_iota(jnp.int32, shape, dim)


def one_hot(mask):
    return jnp.where(mask, 1.0, 0.0).astype(jnp.bfloat16)


def wait_bytes(ref, sem):
    pltpu.make_async_copy(ref, ref, sem).wait()


def target_rows(dest_rows):
    dests = dest_rows.astype(jnp.bfloat16)
    spread = one_hot(iota((128, ROWS), 0) == iota((128, ROWS), 1) % 64)
    wide = dot(dests, spread)
    of_source = iota((SHARDS, ROWS), 0) == iota((SHARDS, ROWS), 1) // 64
    dest = jnp.sum(jnp.where(of_source, wide, 0.0), axis=0, keepdims=True)
    dest_int = dest.astype(jnp.int32)
    named = jnp.where(iota((SHARDS, ROWS), 0) == dest_int, 1.0, 0.0)
    row = iota((ROWS, 128), 0)
    first = one_hot(jnp.logical_and(row // 64 == iota((ROWS, 128), 1), row % 4 == 0))
    has = dot(named.astype(jnp.bfloat16), first)
    earlier = one_hot(iota((128, 128), 0) < iota((128, 128), 1))
    rank = dot(has.astype(jnp.bfloat16), earlier)
    back = one_hot(iota((128, ROWS), 0) == iota((128, ROWS), 1) // 64)
    rank_wide = dot(rank.astype(jnp.bfloat16), back)
    slot = jnp.sum(named * rank_wide, axis=0, keepdims=True).astype(jnp.int32)
    within = iota((1, ROWS), 1) % 4
    return (slot // 4) * SEG + dest_int * 16 + (slot % 4) * 4 + within


def kernel(
    x_hbm, dest_ref, gain_ref, wqkv_hbm, wout_hbm, cot_hbm, enc_hbm, grad_ref,
    xb, xf, send1, recv1, dall, send2, recv2, place, kv, qf, qd, farsend, farrecv,
    wqkv, wfar, wout, normed, qkv, attn, lse, encst, gsend, grecv, ysend, yrecv, ysum, fin,
    bsem, ssem1, rsem1, dssem, drsem, ssem2, rsem2, kvs, kvr, fss, frs,
    gss, grs, yss, yrs, css, crs, xsem, wsem, osem, csem, esem,
):
    me = lax.axis_index("seq")
    dp = lax.axis_index("dp")
    core = lax.rem(me, 2)
    mate = me + 1 - 2 * core
    head = lax.div(me, 2)
    seg_base, attn_base, grad_base = 0, SEG, 2 * SEG

    load_x = pltpu.make_async_copy(x_hbm, xb, xsem)
    load_x.start()
    load_w = pltpu.make_async_copy(wqkv_hbm, wqkv, wsem)
    load_w.start()
    load_o = pltpu.make_async_copy(wout_hbm, wout, osem)
    load_o.start()

    barrier = pltpu.get_barrier_semaphore()

    def greet(step, _):
        pl.semaphore_signal(
            barrier, inc=1, device_id={"seq": peer(me, step)}, device_id_type=MESH
        )
        return 0

    lax.fori_loop(1, SHARDS, greet, 0)
    for step in range(1, SLIDES):
        pl.semaphore_signal(
            barrier, inc=1, device_id={"dp": lax.rem(dp + step, SLIDES)}, device_id_type=MESH
        )

    load_x.wait()

    def widen(index, _):
        rows = pl.ds(pl.multiple_of(index * 256, 256), 256)
        for group in range(GROUPS):
            xf[group, rows, :] = xb[rows, lanes(group)].astype(jnp.float32)
        return 0

    lax.fori_loop(0, ROWS // 256, widen, 0)
    load_c = pltpu.make_async_copy(cot_hbm, xb, csem)
    load_c.start()
    pl.semaphore_wait(barrier, SHARDS - 1 + SLIDES - 1)

    def tell(step, _):
        to = peer(me, step)
        pltpu.make_async_remote_copy(
            src_ref=dest_ref, dst_ref=dall.at[me], send_sem=dssem, recv_sem=drsem,
            device_id={"seq": to}, device_id_type=MESH,
        ).start()
        return 0

    lax.fori_loop(1, SHARDS, tell, 0)
    pltpu.make_async_copy(dest_ref, dall.at[me], drsem).start()

    def pack(to):
        rows = pl.ds(row_class(to), 64, stride=STRIDE)
        for group in range(GROUPS):
            send1[to, :, lanes(group)] = xf[group, rows, :].astype(jnp.bfloat16)

    def scatter(step, _):
        to = peer(me, step)
        pack(to)
        pltpu.make_async_remote_copy(
            src_ref=send1.at[to], dst_ref=recv1.at[me], send_sem=ssem1, recv_sem=rsem1,
            device_id={"seq": to}, device_id_type=MESH,
        ).start()
        return 0

    lax.fori_loop(1, SHARDS, scatter, 0)
    pack(me)
    pltpu.make_async_copy(send1.at[me], recv1.at[me], rsem1).start()

    wait_bytes(dall, drsem)
    target = target_rows(jnp.max(dall[...].astype(jnp.float32), axis=1))

    def build(part, _):
        rows = iota((SEG, ROWS), 0) + part * SEG
        place[part] = one_hot(rows == target)
        return 0

    lax.fori_loop(0, SEGS, build, 0)
    load_w.wait()
    pair_at = lax.div(head, 2) * 128
    for part in range(3):
        at = pl.multiple_of(jnp.minimum(pair_at, WIDTH - 128) + part * WIDTH, 128)
        wfar[:, part * 128 : (part + 1) * 128] = wqkv[:, pl.ds(at, 128)]

    wait_bytes(recv1, rsem1)
    gathered = recv1.reshape(ROWS, WIDTH)

    def regroup(part, _):
        moved = dot(place[part], gathered[...]).astype(jnp.bfloat16)
        send2[part] = moved.reshape(SHARDS, 16, WIDTH)

        def give(step, _):
            to = peer(me, step)
            pltpu.make_async_remote_copy(
                src_ref=send2.at[part, to], dst_ref=recv2.at[part, me],
                send_sem=ssem2.at[part], recv_sem=rsem2.at[part],
                device_id={"seq": to}, device_id_type=MESH,
            ).start()
            return 0

        lax.fori_loop(1, SHARDS, give, 0)
        pltpu.make_async_copy(send2.at[part, me], recv2.at[part, me], rsem2.at[part]).start()
        return 0

    lax.fori_loop(0, SEGS, regroup, 0)

    gain = gain_ref[...]

    @pl.when(head < HEADS)
    def _():
        half = lax.rem(head, 2)
        lane = iota((256, 128), 1)
        mine = lane // HEAD_DIM == half

        def project(index, _):
            rows = pl.ds(pl.multiple_of(index * 256, 256), 256)
            out = dot(normalize(gathered[rows, :].astype(jnp.float32), gain), wfar[...])
            qf[rows, :] = jnp.where(mine, out[:, :128].astype(jnp.bfloat16).astype(jnp.float32) * score_scale, 0.0).astype(jnp.bfloat16)
            kv[core, 0, rows, :] = out[:, 128:256].astype(jnp.bfloat16)
            kv[core, 1, rows, :] = jnp.where(mine, out[:, 256:], 1.0).astype(jnp.bfloat16)
            return 0

        lax.fori_loop(0, ROWS // 256, project, 0)
        swap = pltpu.make_async_remote_copy(
            src_ref=kv.at[core], dst_ref=kv.at[core], send_sem=kvs, recv_sem=kvr,
            device_id={"seq": mate}, device_id_type=MESH,
        )
        swap.start()

        def reorder(part, _):
            at = pl.ds(pl.multiple_of(part * SEG, SEG), SEG)
            qd[at, :] = dot(place[part], qf[...]).astype(jnp.bfloat16)
            return 0

        lax.fori_loop(0, SEGS, reorder, 0)
        swap.wait()
        far_flat = farsend.reshape(ROWS, 128)

        def far(index, _):
            rows = pl.ds(pl.multiple_of(index * 256, 256), 256)
            queries = qd[rows, :]
            scores = [dot_t(queries, kv[side, 0]) for side in range(2)]
            peak = jnp.maximum(
                jnp.max(scores[0], axis=-1, keepdims=True),
                jnp.max(scores[1], axis=-1, keepdims=True),
            )
            accum = jnp.zeros((256, 128), jnp.float32)
            for side in range(2):
                weights = jnp.exp(scores[side] - peak).astype(jnp.bfloat16)
                accum = accum + dot(weights, kv[side, 1])
            total = pltpu.roll(accum, 64, 1)
            mixed = accum / total
            level = peak + jnp.log(jnp.where(mine, 1.0, accum))
            high = level.astype(jnp.bfloat16).astype(jnp.float32)
            tail = jnp.where(lane % 64 < 32, high, level - high)
            far_flat[rows, :] = jnp.where(mine, mixed, tail).astype(jnp.bfloat16)
            return 0

        lax.fori_loop(0, ROWS // 256, far, 0)

        def give_far(step, _):
            to = peer(me, step)
            pltpu.make_async_remote_copy(
                src_ref=farsend.at[:, to], dst_ref=farrecv.at[me], send_sem=fss, recv_sem=frs,
                device_id={"seq": to}, device_id_type=MESH,
            ).start()
            return 0

        lax.fori_loop(1, SHARDS, give_far, 0)
        pltpu.make_async_copy(farsend.at[:, me], farrecv.at[me], frs).start()

    wait_bytes(farrecv, frs)
    load_c.wait()
    load_o.wait()
    low = iota((SEG, 128), 1) < HEAD_DIM
    low_far = iota((16, 128), 1) < HEAD_DIM

    def segment(part, _):
        wait_bytes(recv2.at[part], rsem2.at[part])
        for src in range(SHARDS):
            shift = RATE * (src % 2) + src // 2
            rows = pl.ds(seg_base + shift, 16, stride=STRIDE)
            for group in range(GROUPS):
                xf[group, rows, :] = recv2[part, src, :, lanes(group)].astype(jnp.float32)

        def norm_step(index, _):
            at = pl.multiple_of(index * 128, 128)
            normed[pl.ds(at, 128), :] = normalize(
                jnp.concatenate(
                    [xf[group, pl.ds(seg_base + at, 128), :] for group in range(GROUPS)], axis=1
                ),
                gain,
            )
            return 0

        lax.fori_loop(0, SEG // 128, norm_step, 0)

        def project(index, _):
            cols = pl.ds(pl.multiple_of(index * 384, 384), 384)
            qkv[:, cols] = dot(normed[...], wqkv[:, cols]).astype(jnp.bfloat16)
            return 0

        lax.fori_loop(0, 3 * WIDTH // 384, project, 0)

        def near(pair, _):
            at = pl.multiple_of(pair * 128, 128)
            queries = qkv[:, pl.ds(at, 128)].astype(jnp.float32) * score_scale
            keys = qkv[:, pl.ds(at + WIDTH, 128)]
            values = qkv[:, pl.ds(at + 2 * WIDTH, 128)].astype(jnp.float32)
            accums, peaks = [], []
            for side in range(2):
                mine = low if side == 0 else jnp.logical_not(low)
                scores = dot_t(jnp.where(mine, queries, 0.0).astype(jnp.bfloat16), keys)
                peak = jnp.max(scores, axis=-1, keepdims=True)
                weights = jnp.exp(scores - peak).astype(jnp.bfloat16)
                accums.append(dot(weights, jnp.where(mine, values, 1.0).astype(jnp.bfloat16)))
                peaks.append(peak)
            total = pltpu.roll(jnp.where(low, accums[1], accums[0]), 64, 1)
            xf[pair, pl.ds(attn_base, SEG), :] = jnp.where(low, accums[0], accums[1]) / total
            lse[pair] = jnp.where(low, peaks[0], peaks[1]) + jnp.log(total)
            return 0

        lax.fori_loop(0, PAIRS, near, 0)

        for src in range(FAR_OWNERS):
            number = src // 2
            pair, half = number // 2, number % 2
            shift = RATE * (src % 2) + number
            rows = pl.ds(attn_base + shift, 16, stride=STRIDE)
            near_part = xf[pair, rows, :]
            near_lse = lse[pair, pl.ds(shift, 16, stride=STRIDE), :]
            far_part = farrecv[src, part].astype(jnp.float32)
            other = HEAD_DIM * (1 - half)
            far_lse = far_part[:, other : other + 1] + far_part[:, other + 32 : other + 33]
            top = jnp.maximum(near_lse, far_lse)
            near_share = jnp.exp(near_lse - top)
            far_share = jnp.exp(far_lse - top)
            mixed = (near_share * near_part + far_share * far_part) / (near_share + far_share)
            mine = low_far if half == 0 else jnp.logical_not(low_far)
            xf[pair, rows, :] = jnp.where(mine, mixed, near_part)

        for group in range(GROUPS):
            attn[:, lanes(group)] = xf[group, pl.ds(attn_base, SEG), :].astype(jnp.bfloat16)
        seg_at = pl.multiple_of(part * SEG, SEG)

        def finish(index, _):
            cols = pl.ds(pl.multiple_of(index * 256, 256), 256)
            projected = dot(attn[...], wout[:, cols])
            for sub in range(2):
                part_in = xf[2 * index + sub, pl.ds(seg_base, SEG), :]
                at = pl.multiple_of(index * 256 + sub * 128, 128)
                encst[part, :, pl.ds(at, 128)] = (part_in + projected[:, lanes(sub)]).astype(
                    jnp.bfloat16
                )
            term = lax.dot_general(
                attn[...], xb[pl.ds(seg_at, SEG), cols], (((0,), (0,)), ((), ())),
                preferred_element_type=jnp.float32,
            )
            for sub in range(2):
                held = xf[2 * index + sub, pl.ds(grad_base, WIDTH), :]
                piece = term[:, lanes(sub)]
                xf[2 * index + sub, pl.ds(grad_base, WIDTH), :] = jnp.where(
                    part == 0, piece, held + piece
                )
            return 0

        lax.fori_loop(0, WIDTH // 256, finish, 0)
        pltpu.make_async_copy(
            encst.at[part], enc_hbm.at[pl.ds(seg_at, SEG)], esem.at[part]
        ).start()
        return 0

    lax.fori_loop(0, SEGS, segment, 0)

    for chip in range(SHARDS // 2):
        for side in range(2):
            for group in range(3):
                gsend[2 * chip + side, :, lanes(group)] = xf[
                    3 * side + group, pl.ds(grad_base + 48 * chip, 48), :
                ].astype(jnp.bfloat16)

    def give_grad(step, _):
        to = peer(me, step)
        pltpu.make_async_remote_copy(
            src_ref=gsend.at[to], dst_ref=grecv.at[me], send_sem=gss, recv_sem=grs,
            device_id={"seq": to}, device_id_type=MESH,
        ).start()
        return 0

    lax.fori_loop(1, SHARDS, give_grad, 0)
    pltpu.make_async_copy(gsend.at[me], grecv.at[me], grs).start()
    wait_bytes(grecv, grs)
    ysend[...] = jnp.sum(grecv[...].astype(jnp.float32), axis=0).astype(jnp.bfloat16)
    for step in range(1, SLIDES):
        pltpu.make_async_remote_copy(
            src_ref=ysend, dst_ref=yrecv.at[dp], send_sem=yss, recv_sem=yrs,
            device_id={"dp": lax.rem(dp + step, SLIDES)}, device_id_type=MESH,
        ).start()
    pltpu.make_async_copy(ysend, yrecv.at[dp], yrs).start()
    wait_bytes(yrecv, yrs)
    whole = jnp.sum(yrecv[...].astype(jnp.float32), axis=0)
    ysum[0] = whole[:24]
    ysum[1] = whole[24:]
    last = pltpu.make_async_remote_copy(
        src_ref=ysum.at[1 - core], dst_ref=fin.at[core], send_sem=css, recv_sem=crs,
        device_id={"seq": mate}, device_id_type=MESH,
    )
    last.start()
    fin[core] = ysum[core]
    last.wait()
    grad_ref[:, :384] = fin[0]
    grad_ref[:, 384:] = fin[1]

    wait_bytes(dall.at[pl.ds(0, SHARDS - 1)], dssem)
    wait_bytes(send1.at[pl.ds(0, SHARDS - 1)], ssem1)
    for part in range(SEGS):
        wait_bytes(send2.at[part, pl.ds(0, SHARDS - 1)], ssem2.at[part])
        wait_bytes(encst.at[part], esem.at[part])

    @pl.when(head < HEADS)
    def _():
        wait_bytes(farsend.at[:, pl.ds(0, SHARDS - 1)], fss)

    wait_bytes(gsend.at[pl.ds(0, SHARDS - 1)], gss)
    wait_bytes(yrecv.at[pl.ds(0, SLIDES - 1)], yss)


def body(tile_rows, block_dest, norm_gain, qkv_weight, out_weight, cotangent):
    dests = jnp.pad(jnp.repeat(block_dest, 4, axis=1), ((0, 0), (0, 64)))
    dests = jnp.broadcast_to(dests, (8, 128))
    bf16, f32 = jnp.bfloat16, jnp.float32
    dma = pltpu.SemaphoreType.DMA
    anywhere = pl.BlockSpec(memory_space=pl.ANY)
    vmem = pl.BlockSpec(memory_space=pltpu.VMEM)
    encoded, grad = pl.pallas_call(
        kernel,
        out_shape=(
            jax.ShapeDtypeStruct((ROWS, WIDTH), bf16),
            jax.ShapeDtypeStruct((24, WIDTH), f32),
        ),
        in_specs=[anywhere, vmem, vmem, anywhere, anywhere, anywhere],
        out_specs=(anywhere, vmem),
        scratch_shapes=[
            pltpu.VMEM((ROWS, WIDTH), bf16),
            pltpu.VMEM((GROUPS, ROWS, 128), f32),
            pltpu.VMEM((SHARDS, 64, WIDTH), bf16),
            pltpu.VMEM((SHARDS, 64, WIDTH), bf16),
            pltpu.VMEM((SHARDS, 8, 128), jnp.int32),
            pltpu.VMEM((SEGS, SHARDS, 16, WIDTH), bf16),
            pltpu.VMEM((SEGS, SHARDS, 16, WIDTH), bf16),
            pltpu.VMEM((SEGS, SEG, ROWS), bf16),
            pltpu.VMEM((2, 2, ROWS, 128), bf16),
            pltpu.VMEM((ROWS, 128), bf16),
            pltpu.VMEM((ROWS, 128), bf16),
            pltpu.VMEM((SEGS, SHARDS, 16, 128), bf16),
            pltpu.VMEM((FAR_OWNERS, SEGS, 16, 128), bf16),
            pltpu.VMEM((WIDTH, 3 * WIDTH), bf16),
            pltpu.VMEM((WIDTH, 384), bf16),
            pltpu.VMEM((WIDTH, WIDTH), bf16),
            pltpu.VMEM((SEG, WIDTH), bf16),
            pltpu.VMEM((SEG, 3 * WIDTH), bf16),
            pltpu.VMEM((SEG, WIDTH), bf16),
            pltpu.VMEM((PAIRS, SEG, 128), f32),
            pltpu.VMEM((SEGS, SEG, WIDTH), bf16),
            pltpu.VMEM((SHARDS, 48, 384), bf16),
            pltpu.VMEM((SHARDS, 48, 384), bf16),
            pltpu.VMEM((48, 384), bf16),
            pltpu.VMEM((SLIDES, 48, 384), bf16),
            pltpu.VMEM((2, 24, 384), f32),
            pltpu.VMEM((2, 24, 384), f32),
            dma, dma, dma, dma, dma, dma((SEGS,)), dma((SEGS,)), dma, dma, dma, dma,
            dma, dma, dma, dma, dma, dma, dma, dma, dma, dma, dma((SEGS,)),
        ],
        compiler_params=pltpu.CompilerParams(
            collective_id=0, has_side_effects=True, vmem_limit_bytes=62 * 1024 * 1024
        ),
        name="slide_layer",
    )(
        tile_rows.reshape(ROWS, WIDTH), dests, norm_gain.reshape(1, WIDTH),
        qkv_weight, out_weight, cotangent.reshape(ROWS, WIDTH),
    )
    return encoded.reshape(1, ROWS, WIDTH), grad


def solution(mesh):
    return jax.shard_map(
        body,
        mesh=mesh,
        in_specs=(P("dp", "seq", None), P("dp", "seq"), P(), P(), P(), P("dp", "seq", None)),
        out_specs=(P("dp", "seq", None), P("seq", None)),
        check_vma=False,
    )
```

time: 590 us -> 184 us (0.31); the launches traced: 580 us -> 182 us
  local copies, waits for them, and re-layouts: 216 us -> 7.11 us
  Pallas kernels: 0 us -> 175 us
  waiting for transfers between devices: 130 us -> 0 us
  matrix products: 101 us -> 0 us
  other arithmetic: 84 us -> 0 us
  blocking collectives: 17.8 us -> 0 us
  starting transfers between devices: 16.1 us -> 0 us
  between operations: 14.6 us -> 0.66 us
    pallas_call x0 -> x1, Pallas kernels: none -> 175 us  [body(): pl.pallas_call(kernel, out_shape=(jax.ShapeDtypeStruct((ROWS, WIDTH), bf1...]
    dot_general x17 -> x0, matrix products: 101 us -> none  [the longest x1 14.7 us: body(): jnp.einsum('shqd,shnd->shqn', query_far, key_piece, preferred_element_typ...]
    all_to_all x2 -> x0, waiting for transfers between devices: 65.3 us -> none  [the longest x1 65.3 us: body(): lax.all_to_all(send_blocks, 'seq', split_axis=1, concat_axis=1, tiled=True)]
    reduce_scatter x1 -> x0, waiting for transfers between devices: 65 us -> none  [body(): lax.psum_scatter(grad_slides, 'seq', scatter_dimension=0, tiled=True)]
    unnamed x2 -> x0, other arithmetic: 48.9 us -> none
    convert_element_type x5 -> x0, local copies, waits for them, and re-layouts: 46.8 us -> none  [the longest x1 31 us: body(): send_blocks = jnp.einsum('spj,sjx->spx', placing, blocks, preferred_eleme...]
    broadcast_in_dim x7 -> x4, local copies, waits for them, and re-layouts: 44 us -> 1.41 us  [the longest x2 0.81 us: body(): dests = jnp.pad(jnp.repeat(block_dest, 4, axis=1), ((0, 0), (0, 64)))]
    unnamed x20 -> x4, local copies, waits for them, and re-layouts: 39.3 us -> 4.42 us
  transfers between devices with their start and end apart: 4 -> 0, of which waited for: 2 -> 0; matrix products, arithmetic and copies ran while one was open for 46% -> 0% of each run, Pallas kernels for 0% -> 0%
where the time goes in v1:
time: 184 us; the launch traced here: 182 us
  Pallas kernels  175 us (95%)
  local copies, waits for them, and re-layouts  7.11 us (4%)
    pallas_call x1, Pallas kernels, body(): pl.pallas_call(kernel, out_shape=(jax.ShapeDtypeStruct((ROWS, WIDTH), bf1...  175 us
    unnamed x4, local copies, waits for them, and re-layouts  4.42 us

profile of v1, /device:TPU:0, one launch (start us, length us, event | category | flops | bytes accessed | tf_op | source)
XLA Modules:
  0.0 182.5 jit_solution(3283153165190457502)
XLA Ops:
  0.6 1.3 reshape.22.gain_ref
  1.9 0.7 broadcast_in_dim.12
  2.6 0.1 broadcast_in_dim.13
  2.7 0.6 broadcast_in_dim.15.dest_ref
  3.3 174.7 %slide_layer.1 = (bf16[2048,768]{1,0:T(8,128)(2,1)}, f32[24,768]{1,0:T(8,128)}) custom-call(bf16[2048,768]{1,0:T(8,128)(2,1)} %bitcast.7, s32[8,128]{1,0:T(8,128)} %broadcast_in_dim.15.dest_ref, f32[1,768]{1,0:T(1,128)} %reshape.22.gain_ref, bf16[768,2304]{1,0:T(8,128)(2,1)} %wqkv_hbm.1, bf16[768,768]{1,0:T(8,128)(2,1)} %wout_hbm.1, bf16[2048,768]{1,0:T(8,128)(2,1)} %bitcast.8), custom_call_target="tpu_custom_call" | custom-call | tf_op jit(solution)/shard_map/slide_layer/pallas_call | solution.py:434
  178.0 0.0 copy-start
  178.0 3.8 %copy.10 = bf16[1,2048,768]{2,1,0:T(8,128)(2,1)} copy(bf16[1,2048,768]{2,1,0:T(8,128)(2,1)} %bitcast.6) | data formatting | bytes 6291456
  181.8 0.0 copy-done
  181.8 0.6 copy.11
  (1 shorter events, 0.0 us)
Async XLA Ops:
  178.0 3.8 %copy-start = (f32[24,768]{1,0:T(8,128)S(1)}, f32[24,768]{1,0:T(8,128)}, u32[]{:S(2)}) copy-start(f32[24,768]{1,0:T(8,128)} %get-tuple-element.9) | copy-start | bytes 221188

commit v2 on v1

--- a/solution.py
+++ b/solution.py
@@ -43,6 +43,14 @@
     return lax.rem(z + dz, 4) * 8 + lax.rem(x + dx, 4) * 2 + lax.rem(c + dc, 2)
 
 
+def origin(me, step):
+    z, x, c = lax.div(me, 8), lax.rem(lax.div(me, 2), 4), lax.rem(me, 2)
+    dz = lax.rem(step, 4)
+    dx = lax.rem(step + lax.div(step, 8), 4)
+    dc = lax.rem(lax.div(step, 4), 2)
+    return lax.rem(z + 4 - dz, 4) * 8 + lax.rem(x + 4 - dx, 4) * 2 + lax.rem(c + 2 - dc, 2)
+
+
 def normalize(values, gain):
     center = values - jnp.mean(values, axis=-1, keepdims=True)
     spread = jnp.mean(center * center, axis=-1, keepdims=True)
@@ -69,7 +77,7 @@
     pltpu.make_async_copy(ref, ref, sem).wait()
 
 
-def target_rows(dest_rows):
+def target_rows(me, dest_rows):
     dests = dest_rows.astype(jnp.bfloat16)
     spread = one_hot(iota((128, ROWS), 0) == iota((128, ROWS), 1) % 64)
     wide = dot(dests, spread)
@@ -80,7 +88,7 @@
     row = iota((ROWS, 128), 0)
     first = one_hot(jnp.logical_and(row // 64 == iota((ROWS, 128), 1), row % 4 == 0))
     has = dot(named.astype(jnp.bfloat16), first)
-    earlier = one_hot(iota((128, 128), 0) < iota((128, 128), 1))
+    earlier = one_hot(origin(me, iota((128, 128), 0)) < origin(me, iota((128, 128), 1)))
     rank = dot(has.astype(jnp.bfloat16), earlier)
     back = one_hot(iota((128, ROWS), 0) == iota((128, ROWS), 1) // 64)
     rank_wide = dot(rank.astype(jnp.bfloat16), back)
@@ -92,9 +100,9 @@
 def kernel(
     x_hbm, dest_ref, gain_ref, wqkv_hbm, wout_hbm, cot_hbm, enc_hbm, grad_ref,
     xb, xf, send1, recv1, dall, send2, recv2, place, kv, qf, qd, farsend, farrecv,
-    wqkv, wfar, wout, normed, qkv, attn, lse, encst, gsend, grecv, ysend, yrecv, ysum, fin,
-    bsem, ssem1, rsem1, dssem, drsem, ssem2, rsem2, kvs, kvr, fss, frs,
-    gss, grs, yss, yrs, css, crs, xsem, wsem, osem, csem, esem,
+    wqkv, wfar, wout, normed, qkv, attn, lse, encst, gsend, gmate, gpart, grecv, ysend, yrecv, ysum, fin,
+    ssem1, rsem1, dssem, drsem, ssem2, rsem2, kvs, kvr, fss, frs,
+    jss, jrs, gss, grs, yss, yrs, css, crs, xsem, wsem, osem, csem, esem,
 ):
     me = lax.axis_index("seq")
     dp = lax.axis_index("dp")
@@ -140,13 +148,13 @@
     def tell(step, _):
         to = peer(me, step)
         pltpu.make_async_remote_copy(
-            src_ref=dest_ref, dst_ref=dall.at[me], send_sem=dssem, recv_sem=drsem,
+            src_ref=dest_ref, dst_ref=dall.at[step], send_sem=dssem, recv_sem=drsem,
             device_id={"seq": to}, device_id_type=MESH,
         ).start()
         return 0
 
     lax.fori_loop(1, SHARDS, tell, 0)
-    pltpu.make_async_copy(dest_ref, dall.at[me], drsem).start()
+    pltpu.make_async_copy(dest_ref, dall.at[0], drsem).start()
 
     def pack(to):
         rows = pl.ds(row_class(to), 64, stride=STRIDE)
@@ -157,17 +165,18 @@
         to = peer(me, step)
         pack(to)
         pltpu.make_async_remote_copy(
-            src_ref=send1.at[to], dst_ref=recv1.at[me], send_sem=ssem1, recv_sem=rsem1,
+            src_ref=send1.at[to], dst_ref=recv1.at[step], send_sem=ssem1,
+            recv_sem=rsem1.at[lax.div(step, 8)],
             device_id={"seq": to}, device_id_type=MESH,
         ).start()
         return 0
 
     lax.fori_loop(1, SHARDS, scatter, 0)
     pack(me)
-    pltpu.make_async_copy(send1.at[me], recv1.at[me], rsem1).start()
+    pltpu.make_async_copy(send1.at[me], recv1.at[0], rsem1.at[0]).start()
 
     wait_bytes(dall, drsem)
-    target = target_rows(jnp.max(dall[...].astype(jnp.float32), axis=1))
+    target = target_rows(me, jnp.max(dall[...].astype(jnp.float32), axis=1))
 
     def build(part, _):
         rows = iota((SEG, ROWS), 0) + part * SEG
@@ -181,12 +190,44 @@
         at = pl.multiple_of(jnp.minimum(pair_at, WIDTH - 128) + part * WIDTH, 128)
         wfar[:, part * 128 : (part + 1) * 128] = wqkv[:, pl.ds(at, 128)]
 
-    wait_bytes(recv1, rsem1)
     gathered = recv1.reshape(ROWS, WIDTH)
-
-    def regroup(part, _):
-        moved = dot(place[part], gathered[...]).astype(jnp.bfloat16)
-        send2[part] = moved.reshape(SHARDS, 16, WIDTH)
+    gain = gain_ref[...]
+    half = lax.rem(head, 2)
+
+    def far_project(group):
+        mine = iota((SEG, 128), 1) // HEAD_DIM == half
+        rows = slice(group * SEG, group * SEG + SEG)
+        out = dot(normalize(gathered[rows, :].astype(jnp.float32), gain), wfar[...])
+        out = out.astype(jnp.bfloat16)
+        zero, one = jnp.bfloat16(0.0), jnp.bfloat16(1.0)
+        qf[rows, :] = jnp.where(mine, out[:, :128] * jnp.bfloat16(score_scale), zero)
+        kv[core, 0, rows, :] = out[:, 128:256]
+        kv[core, 1, rows, :] = jnp.where(mine, out[:, 256:], one)
+
+    def moved(part, group):
+        rows = slice(group * SEG, group * SEG + SEG)
+        return dot(place[part, :, rows], gathered[rows, :])
+
+    for group in range(SEGS - 1):
+        wait_bytes(recv1.at[pl.ds(8 * group, 8)], rsem1.at[group])
+
+        def regroup(part, _, group=group):
+            term = moved(part, group)
+            at = pl.ds(pl.multiple_of(part * SEG, SEG), SEG)
+            for cols in range(GROUPS):
+                piece = term[:, lanes(cols)]
+                xf[cols, at, :] = piece if group == 0 else xf[cols, at, :] + piece
+            return 0
+
+        lax.fori_loop(0, SEGS, regroup, 0)
+        pl.when(head < HEADS)(functools.partial(far_project, group))
+
+    def deliver(part, _):
+        term = moved(part, SEGS - 1)
+        at = pl.ds(pl.multiple_of(part * SEG, SEG), SEG)
+        for cols in range(GROUPS):
+            piece = (xf[cols, at, :] + term[:, lanes(cols)]).astype(jnp.bfloat16)
+            send2[part, :, :, lanes(cols)] = piece.reshape(SHARDS, 16, 128)
 
         def give(step, _):
             to = peer(me, step)
@@ -201,25 +242,12 @@
         pltpu.make_async_copy(send2.at[part, me], recv2.at[part, me], rsem2.at[part]).start()
         return 0
 
-    lax.fori_loop(0, SEGS, regroup, 0)
-
-    gain = gain_ref[...]
+    wait_bytes(recv1.at[pl.ds(24, 8)], rsem1.at[SEGS - 1])
+    lax.fori_loop(0, 2, deliver, 0)
 
     @pl.when(head < HEADS)
     def _():
-        half = lax.rem(head, 2)
-        lane = iota((256, 128), 1)
-        mine = lane // HEAD_DIM == half
-
-        def project(index, _):
-            rows = pl.ds(pl.multiple_of(index * 256, 256), 256)
-            out = dot(normalize(gathered[rows, :].astype(jnp.float32), gain), wfar[...])
-            qf[rows, :] = jnp.where(mine, out[:, :128].astype(jnp.bfloat16).astype(jnp.float32) * score_scale, 0.0).astype(jnp.bfloat16)
-            kv[core, 0, rows, :] = out[:, 128:256].astype(jnp.bfloat16)
-            kv[core, 1, rows, :] = jnp.where(mine, out[:, 256:], 1.0).astype(jnp.bfloat16)
-            return 0
-
-        lax.fori_loop(0, ROWS // 256, project, 0)
+        far_project(SEGS - 1)
         swap = pltpu.make_async_remote_copy(
             src_ref=kv.at[core], dst_ref=kv.at[core], send_sem=kvs, recv_sem=kvr,
             device_id={"seq": mate}, device_id_type=MESH,
@@ -234,19 +262,27 @@
         lax.fori_loop(0, SEGS, reorder, 0)
         swap.wait()
         far_flat = farsend.reshape(ROWS, 128)
+        lane = iota((SEG, 128), 1)
+        mine = lane // HEAD_DIM == half
 
         def far(index, _):
-            rows = pl.ds(pl.multiple_of(index * 256, 256), 256)
+            rows = pl.ds(pl.multiple_of(index * SEG, SEG), SEG)
             queries = qd[rows, :]
-            scores = [dot_t(queries, kv[side, 0]) for side in range(2)]
-            peak = jnp.maximum(
-                jnp.max(scores[0], axis=-1, keepdims=True),
-                jnp.max(scores[1], axis=-1, keepdims=True),
-            )
-            accum = jnp.zeros((256, 128), jnp.float32)
-            for side in range(2):
-                weights = jnp.exp(scores[side] - peak).astype(jnp.bfloat16)
-                accum = accum + dot(weights, kv[side, 1])
+            blocks = [(side, slice(at, at + SEG)) for side in range(2) for at in range(0, ROWS, SEG)]
+            upcoming = dot_t(queries, kv[0, 0, blocks[0][1], :])
+            peak = accum = None
+            for number, (side, keys) in enumerate(blocks):
+                scores = upcoming
+                if number + 1 < len(blocks):
+                    after, cut = blocks[number + 1]
+                    upcoming = dot_t(queries, kv[after, 0, cut, :])
+                top = jnp.max(scores, axis=-1, keepdims=True)
+                if number:
+                    top = jnp.maximum(peak, top)
+                    accum = accum * jnp.exp(peak - top)
+                term = dot(jnp.exp(scores - top).astype(jnp.bfloat16), kv[side, 1, keys, :])
+                accum = accum + term if number else term
+                peak = top
             total = pltpu.roll(accum, 64, 1)
             mixed = accum / total
             level = peak + jnp.log(jnp.where(mine, 1.0, accum))
@@ -255,7 +291,7 @@
             far_flat[rows, :] = jnp.where(mine, mixed, tail).astype(jnp.bfloat16)
             return 0
 
-        lax.fori_loop(0, ROWS // 256, far, 0)
+        lax.fori_loop(0, SEGS, far, 0)
 
         def give_far(step, _):
             to = peer(me, step)
@@ -268,6 +304,7 @@
         lax.fori_loop(1, SHARDS, give_far, 0)
         pltpu.make_async_copy(farsend.at[:, me], farrecv.at[me], frs).start()
 
+    lax.fori_loop(2, SEGS, deliver, 0)
     wait_bytes(farrecv, frs)
     load_c.wait()
     load_o.wait()
@@ -282,44 +319,53 @@
             for group in range(GROUPS):
                 xf[group, rows, :] = recv2[part, src, :, lanes(group)].astype(jnp.float32)
 
-        def norm_step(index, _):
-            at = pl.multiple_of(index * 128, 128)
-            normed[pl.ds(at, 128), :] = normalize(
+        for at in range(0, SEG, 128):
+            normed[at : at + 128, :] = normalize(
                 jnp.concatenate(
                     [xf[group, pl.ds(seg_base + at, 128), :] for group in range(GROUPS)], axis=1
                 ),
                 gain,
             )
-            return 0
-
-        lax.fori_loop(0, SEG // 128, norm_step, 0)
-
-        def project(index, _):
-            cols = pl.ds(pl.multiple_of(index * 384, 384), 384)
-            qkv[:, cols] = dot(normed[...], wqkv[:, cols]).astype(jnp.bfloat16)
-            return 0
-
-        lax.fori_loop(0, 3 * WIDTH // 384, project, 0)
-
-        def near(pair, _):
-            at = pl.multiple_of(pair * 128, 128)
-            queries = qkv[:, pl.ds(at, 128)].astype(jnp.float32) * score_scale
-            keys = qkv[:, pl.ds(at + WIDTH, 128)]
-            values = qkv[:, pl.ds(at + 2 * WIDTH, 128)].astype(jnp.float32)
-            accums, peaks = [], []
-            for side in range(2):
-                mine = low if side == 0 else jnp.logical_not(low)
-                scores = dot_t(jnp.where(mine, queries, 0.0).astype(jnp.bfloat16), keys)
-                peak = jnp.max(scores, axis=-1, keepdims=True)
-                weights = jnp.exp(scores - peak).astype(jnp.bfloat16)
-                accums.append(dot(weights, jnp.where(mine, values, 1.0).astype(jnp.bfloat16)))
-                peaks.append(peak)
-            total = pltpu.roll(jnp.where(low, accums[1], accums[0]), 64, 1)
-            xf[pair, pl.ds(attn_base, SEG), :] = jnp.where(low, accums[0], accums[1]) / total
-            lse[pair] = jnp.where(low, peaks[0], peaks[1]) + jnp.log(total)
-            return 0
-
-        lax.fori_loop(0, PAIRS, near, 0)
+
+        def project(index):
+            for kind in range(3):
+                cols = slice(kind * WIDTH + index * 256, kind * WIDTH + index * 256 + 256)
+                qkv[:, cols] = dot(normed[...], wqkv[:, cols]).astype(jnp.bfloat16)
+
+        def operands(number):
+            pair, side = number // 2, number % 2
+            mine = low if side == 0 else jnp.logical_not(low)
+            queries = qkv[:, lanes(pair)] * jnp.bfloat16(score_scale)
+            values = qkv[:, lanes(pair + 2 * PAIRS)]
+            return (
+                jnp.where(mine, queries, jnp.zeros_like(queries)),
+                qkv[:, lanes(pair + PAIRS)],
+                jnp.where(mine, values, jnp.ones_like(values)),
+            )
+
+        def start_head(number):
+            queries, keys, values = operands(number)
+            return dot_t(queries, keys), values
+
+        project(0)
+        upcoming = start_head(0)
+        kept = []
+        for number in range(HEADS):
+            scores, values = upcoming
+            if number % 4 == 0 and number + 4 < HEADS:
+                project(number // 4 + 1)
+            if number + 1 < HEADS:
+                upcoming = start_head(number + 1)
+            peak = jnp.max(scores, axis=-1, keepdims=True)
+            weights = jnp.exp(scores - peak).astype(jnp.bfloat16)
+            kept.append((dot(weights, values), peak))
+            if number % 2:
+                (accum0, peak0), (accum1, peak1) = kept
+                kept = []
+                total = pltpu.roll(jnp.where(low, accum1, accum0), 64, 1)
+                pair = number // 2
+                xf[pair, pl.ds(attn_base, SEG), :] = jnp.where(low, accum0, accum1) / total
+                lse[pair] = jnp.where(low, peak0, peak1) + jnp.log(total)
 
         for src in range(FAR_OWNERS):
             number = src // 2
@@ -342,28 +388,22 @@
             attn[:, lanes(group)] = xf[group, pl.ds(attn_base, SEG), :].astype(jnp.bfloat16)
         seg_at = pl.multiple_of(part * SEG, SEG)
 
-        def finish(index, _):
-            cols = pl.ds(pl.multiple_of(index * 256, 256), 256)
+        for index in range(3):
+            cols = slice(index * 256, index * 256 + 256)
             projected = dot(attn[...], wout[:, cols])
-            for sub in range(2):
-                part_in = xf[2 * index + sub, pl.ds(seg_base, SEG), :]
-                at = pl.multiple_of(index * 256 + sub * 128, 128)
-                encst[part, :, pl.ds(at, 128)] = (part_in + projected[:, lanes(sub)]).astype(
-                    jnp.bfloat16
-                )
             term = lax.dot_general(
                 attn[...], xb[pl.ds(seg_at, SEG), cols], (((0,), (0,)), ((), ())),
                 preferred_element_type=jnp.float32,
             )
             for sub in range(2):
-                held = xf[2 * index + sub, pl.ds(grad_base, WIDTH), :]
+                group = 2 * index + sub
+                encst[part, :, lanes(group)] = (
+                    xf[group, pl.ds(seg_base, SEG), :] + projected[:, lanes(sub)]
+                ).astype(jnp.bfloat16)
+                held = xf[group, pl.ds(grad_base, WIDTH), :]
                 piece = term[:, lanes(sub)]
-                xf[2 * index + sub, pl.ds(grad_base, WIDTH), :] = jnp.where(
-                    part == 0, piece, held + piece
-                )
-            return 0
-
-        lax.fori_loop(0, WIDTH // 256, finish, 0)
+                xf[group, pl.ds(grad_base, WIDTH), :] = jnp.where(part == 0, piece, held + piece)
+
         pltpu.make_async_copy(
             encst.at[part], enc_hbm.at[pl.ds(seg_at, SEG)], esem.at[part]
         ).start()
@@ -371,23 +411,32 @@
 
     lax.fori_loop(0, SEGS, segment, 0)
 
-    for chip in range(SHARDS // 2):
-        for side in range(2):
-            for group in range(3):
-                gsend[2 * chip + side, :, lanes(group)] = xf[
-                    3 * side + group, pl.ds(grad_base + 48 * chip, 48), :
-                ].astype(jnp.bfloat16)
+    for side in range(2):
+        for group in range(3):
+            gsend[side, :, lanes(group)] = xf[
+                3 * side + group, pl.ds(grad_base, WIDTH), :
+            ].astype(jnp.bfloat16)
+    join = pltpu.make_async_remote_copy(
+        src_ref=gsend.at[1 - core], dst_ref=gmate, send_sem=jss, recv_sem=jrs,
+        device_id={"seq": mate}, device_id_type=MESH,
+    )
+    join.start()
+    join.wait()
+    both = gsend[core].astype(jnp.float32) + gmate[...].astype(jnp.float32)
+    gpart[...] = both.astype(jnp.bfloat16).reshape(SHARDS // 2, 48, 384)
 
     def give_grad(step, _):
-        to = peer(me, step)
+        to = lax.rem(lax.div(me, 8) + lax.rem(step, 4), 4) * 8 + lax.rem(
+            lax.rem(lax.div(me, 2), 4) + lax.rem(step + lax.div(step, 4), 4), 4
+        ) * 2 + core
         pltpu.make_async_remote_copy(
-            src_ref=gsend.at[to], dst_ref=grecv.at[me], send_sem=gss, recv_sem=grs,
+            src_ref=gpart.at[lax.div(to, 2)], dst_ref=grecv.at[head], send_sem=gss, recv_sem=grs,
             device_id={"seq": to}, device_id_type=MESH,
         ).start()
         return 0
 
-    lax.fori_loop(1, SHARDS, give_grad, 0)
-    pltpu.make_async_copy(gsend.at[me], grecv.at[me], grs).start()
+    lax.fori_loop(1, SHARDS // 2, give_grad, 0)
+    pltpu.make_async_copy(gpart.at[head], grecv.at[head], grs).start()
     wait_bytes(grecv, grs)
     ysend[...] = jnp.sum(grecv[...].astype(jnp.float32), axis=0).astype(jnp.bfloat16)
     for step in range(1, SLIDES):
@@ -420,7 +469,7 @@
     def _():
         wait_bytes(farsend.at[:, pl.ds(0, SHARDS - 1)], fss)
 
-    wait_bytes(gsend.at[pl.ds(0, SHARDS - 1)], gss)
+    wait_bytes(gpart.at[pl.ds(0, SHARDS // 2 - 1)], gss)
     wait_bytes(yrecv.at[pl.ds(0, SLIDES - 1)], yss)
 
 
@@ -461,13 +510,15 @@
             pltpu.VMEM((SEG, WIDTH), bf16),
             pltpu.VMEM((PAIRS, SEG, 128), f32),
             pltpu.VMEM((SEGS, SEG, WIDTH), bf16),
-            pltpu.VMEM((SHARDS, 48, 384), bf16),
-            pltpu.VMEM((SHARDS, 48, 384), bf16),
+            pltpu.VMEM((2, WIDTH, 384), bf16),
+            pltpu.VMEM((WIDTH, 384), bf16),
+            pltpu.VMEM((SHARDS // 2, 48, 384), bf16),
+            pltpu.VMEM((SHARDS // 2, 48, 384), bf16),
             pltpu.VMEM((48, 384), bf16),
             pltpu.VMEM((SLIDES, 48, 384), bf16),
             pltpu.VMEM((2, 24, 384), f32),
             pltpu.VMEM((2, 24, 384), f32),
-            dma, dma, dma, dma, dma, dma((SEGS,)), dma((SEGS,)), dma, dma, dma, dma,
+            dma, dma((SEGS,)), dma, dma, dma((SEGS,)), dma((SEGS,)), dma, dma, dma, dma, dma, dma,
             dma, dma, dma, dma, dma, dma, dma, dma, dma, dma, dma((SEGS,)),
         ],
         compiler_params=pltpu.CompilerParams(

time: 184 us -> 142 us (0.77)
  Pallas kernels: 175 us -> 132 us
    pallas_call x1, Pallas kernels: 175 us -> 132 us  [body(): pl.pallas_call(kernel, out_shape=(jax.ShapeDtypeStruct((ROWS, WIDTH), bf1...]
where the time goes in v2:
time: 142 us; the launch traced here: 139 us
  Pallas kernels  132 us (93%)
  local copies, waits for them, and re-layouts  7.11 us (5%)
    pallas_call x1, Pallas kernels, body(): pl.pallas_call(kernel, out_shape=(jax.ShapeDtypeStruct((ROWS, WIDTH), bf1...  132 us
    unnamed x4, local copies, waits for them, and re-layouts  4.42 us

profile of v2, /device:TPU:0, one launch (start us, length us, event | category | flops | bytes accessed | tf_op | source)
XLA Modules:
  0.0 139.4 jit_solution(14770229961469775263)
XLA Ops:
  0.6 1.3 reshape.22.gain_ref
  1.9 0.7 broadcast_in_dim.12
  2.6 0.1 broadcast_in_dim.13
  2.7 0.6 broadcast_in_dim.15.dest_ref
  3.3 131.6 %slide_layer.1 = (bf16[2048,768]{1,0:T(8,128)(2,1)}, f32[24,768]{1,0:T(8,128)}) custom-call(bf16[2048,768]{1,0:T(8,128)(2,1)} %bitcast.7, s32[8,128]{1,0:T(8,128)} %broadcast_in_dim.15.dest_ref, f32[1,768]{1,0:T(1,128)} %reshape.22.gain_ref, bf16[768,2304]{1,0:T(8,128)(2,1)} %wqkv_hbm.1, bf16[768,768]{1,0:T(8,128)(2,1)} %wout_hbm.1, bf16[2048,768]{1,0:T(8,128)(2,1)} %bitcast.8), custom_call_target="tpu_custom_call" | custom-call | tf_op jit(solution)/shard_map/slide_layer/pallas_call | solution.py:483
  134.9 0.0 copy-start
  134.9 3.8 %copy.10 = bf16[1,2048,768]{2,1,0:T(8,128)(2,1)} copy(bf16[1,2048,768]{2,1,0:T(8,128)(2,1)} %bitcast.6) | data formatting | bytes 6291456
  138.7 0.0 copy-done
  138.7 0.6 copy.11
  (1 shorter events, 0.0 us)
Async XLA Ops:
  134.9 3.8 %copy-start = (f32[24,768]{1,0:T(8,128)S(1)}, f32[24,768]{1,0:T(8,128)}, u32[]{:S(2)}) copy-start(f32[24,768]{1,0:T(8,128)} %get-tuple-element.9) | copy-start | bytes 221188

commit v3 on v2

--- a/solution.py
+++ b/solution.py
@@ -99,8 +99,8 @@
 
 def kernel(
     x_hbm, dest_ref, gain_ref, wqkv_hbm, wout_hbm, cot_hbm, enc_hbm, grad_ref,
-    xb, xf, send1, recv1, dall, send2, recv2, place, kv, qf, qd, farsend, farrecv,
-    wqkv, wfar, wout, normed, qkv, attn, lse, encst, gsend, gmate, gpart, grecv, ysend, yrecv, ysum, fin,
+    xb, xf, send1, recv1, dsend, dall, send2, recv2, place, ordered, classed, kv, qf, fout, farsend, farrecv,
+    wqkv, wfar, wout, normed, qkv, mix, lse, grad, gsend, gmate, gpart, grecv, ysend, yrecv, ysum, fin,
     ssem1, rsem1, dssem, drsem, ssem2, rsem2, kvs, kvr, fss, frs,
     jss, jrs, gss, grs, yss, yrs, css, crs, xsem, wsem, osem, csem, esem,
 ):
@@ -109,10 +109,15 @@
     core = lax.rem(me, 2)
     mate = me + 1 - 2 * core
     head = lax.div(me, 2)
-    seg_base, attn_base, grad_base = 0, SEG, 2 * SEG
-
-    load_x = pltpu.make_async_copy(x_hbm, xb, xsem)
-    load_x.start()
+
+    load_x = [
+        pltpu.make_async_copy(
+            x_hbm.at[pl.ds(at, SEG)], xb.at[pl.ds(at, SEG)], xsem.at[at // SEG]
+        )
+        for at in range(0, ROWS, SEG)
+    ]
+    for load in load_x:
+        load.start()
     load_w = pltpu.make_async_copy(wqkv_hbm, wqkv, wsem)
     load_w.start()
     load_o = pltpu.make_async_copy(wout_hbm, wout, osem)
@@ -132,15 +137,18 @@
             barrier, inc=1, device_id={"dp": lax.rem(dp + step, SLIDES)}, device_id_type=MESH
         )
 
-    load_x.wait()
+    spread = one_hot(iota((16, 128), 0) == iota((16, 128), 1) // 4)
+    dests = dot(dest_ref[...].astype(jnp.float32).astype(jnp.bfloat16), spread)
+    dsend[...] = jnp.broadcast_to(dests, (8, 128)).astype(jnp.int32)
 
     def widen(index, _):
-        rows = pl.ds(pl.multiple_of(index * 256, 256), 256)
+        wait_bytes(xb.at[pl.ds(0, SEG)], xsem.at[index])
+        rows = pl.ds(pl.multiple_of(index * SEG, SEG), SEG)
         for group in range(GROUPS):
             xf[group, rows, :] = xb[rows, lanes(group)].astype(jnp.float32)
         return 0
 
-    lax.fori_loop(0, ROWS // 256, widen, 0)
+    lax.fori_loop(0, SEGS, widen, 0)
     load_c = pltpu.make_async_copy(cot_hbm, xb, csem)
     load_c.start()
     pl.semaphore_wait(barrier, SHARDS - 1 + SLIDES - 1)
@@ -148,13 +156,13 @@
     def tell(step, _):
         to = peer(me, step)
         pltpu.make_async_remote_copy(
-            src_ref=dest_ref, dst_ref=dall.at[step], send_sem=dssem, recv_sem=drsem,
+            src_ref=dsend, dst_ref=dall.at[step], send_sem=dssem, recv_sem=drsem,
             device_id={"seq": to}, device_id_type=MESH,
         ).start()
         return 0
 
     lax.fori_loop(1, SHARDS, tell, 0)
-    pltpu.make_async_copy(dest_ref, dall.at[0], drsem).start()
+    pltpu.make_async_copy(dsend, dall.at[0], drsem).start()
 
     def pack(to):
         rows = pl.ds(row_class(to), 64, stride=STRIDE)
@@ -184,6 +192,17 @@
         return 0
 
     lax.fori_loop(0, SEGS, build, 0)
+    row, col = iota((SEG, SEG), 0), iota((SEG, SEG), 1)
+    ordered[...] = one_hot(col == 32 * (row % RATE) + 16 * (row % STRIDE // RATE) + row // STRIDE)
+    classed[...] = one_hot(col == STRIDE * (row % 16) + row_class(row // 16))
+    load_c.wait()
+
+    def class_order(part, _):
+        rows = pl.ds(pl.multiple_of(part * SEG, SEG), SEG)
+        xb[rows, :] = dot(classed[...], xb[rows, :]).astype(jnp.bfloat16)
+        return 0
+
+    lax.fori_loop(0, SEGS, class_order, 0)
     load_w.wait()
     pair_at = lax.div(head, 2) * 128
     for part in range(3):
@@ -191,7 +210,7 @@
         wfar[:, part * 128 : (part + 1) * 128] = wqkv[:, pl.ds(at, 128)]
 
     gathered = recv1.reshape(ROWS, WIDTH)
-    gain = gain_ref[...]
+    gain = gain_ref[...].reshape(1, WIDTH)
     half = lax.rem(head, 2)
 
     def far_project(group):
@@ -204,6 +223,42 @@
         kv[core, 0, rows, :] = out[:, 128:256]
         kv[core, 1, rows, :] = jnp.where(mine, out[:, 256:], one)
 
+    def swap(stage):
+        rows = pl.ds(stage * 3 * SEG, 3 * SEG if stage == 0 else SEG)
+        return pltpu.make_async_remote_copy(
+            src_ref=kv.at[core, :, rows], dst_ref=kv.at[core, :, rows],
+            send_sem=kvs.at[stage], recv_sem=kvr.at[stage],
+            device_id={"seq": mate}, device_id_type=MESH,
+        )
+
+    blocks = [(side, slice(at, at + SEG)) for side in range(2) for at in range(0, ROWS, SEG)]
+
+    def far_blocks(queries):
+        accum = peak = None
+        upcoming = dot_t(queries, kv[blocks[0][0], 0, blocks[0][1], :])
+        for number, (side, keys) in enumerate(blocks):
+            scores = upcoming
+            if number + 1 < len(blocks):
+                after, cut = blocks[number + 1]
+                upcoming = dot_t(queries, kv[after, 0, cut, :])
+            top = jnp.max(scores, axis=-1, keepdims=True)
+            if peak is not None:
+                top = jnp.maximum(peak, top)
+                accum = accum * jnp.exp(peak - top)
+            term = dot(jnp.exp(scores - top).astype(jnp.bfloat16), kv[side, 1, keys, :])
+            accum = term if accum is None else accum + term
+            peak = top
+        return accum, peak
+
+    def far_result(accum, peak):
+        lane = iota((SEG, 128), 1)
+        mine = lane // HEAD_DIM == half
+        mixed = accum / pltpu.roll(accum, 64, 1)
+        level = peak + jnp.log(jnp.where(mine, 1.0, accum))
+        high = level.astype(jnp.bfloat16).astype(jnp.float32)
+        tail = jnp.where(lane % 64 < 32, high, level - high)
+        return jnp.where(mine, mixed, tail).astype(jnp.bfloat16)
+
     def moved(part, group):
         rows = slice(group * SEG, group * SEG + SEG)
         return dot(place[part, :, rows], gathered[rows, :])
@@ -219,8 +274,13 @@
                 xf[cols, at, :] = piece if group == 0 else xf[cols, at, :] + piece
             return 0
 
+        @pl.when(head < HEADS)
+        def _(group=group):
+            far_project(group)
+            if group == SEGS - 2:
+                swap(0).start()
+
         lax.fori_loop(0, SEGS, regroup, 0)
-        pl.when(head < HEADS)(functools.partial(far_project, group))
 
     def deliver(part, _):
         term = moved(part, SEGS - 1)
@@ -243,55 +303,20 @@
         return 0
 
     wait_bytes(recv1.at[pl.ds(24, 8)], rsem1.at[SEGS - 1])
-    lax.fori_loop(0, 2, deliver, 0)
-
-    @pl.when(head < HEADS)
-    def _():
-        far_project(SEGS - 1)
-        swap = pltpu.make_async_remote_copy(
-            src_ref=kv.at[core], dst_ref=kv.at[core], send_sem=kvs, recv_sem=kvr,
-            device_id={"seq": mate}, device_id_type=MESH,
-        )
-        swap.start()
-
+
+    def far(index, _):
+        rows = pl.ds(pl.multiple_of(index * SEG, SEG), SEG)
+        fout[rows, :] = far_result(*far_blocks(qf[rows, :]))
+        return 0
+
+    def return_far():
         def reorder(part, _):
-            at = pl.ds(pl.multiple_of(part * SEG, SEG), SEG)
-            qd[at, :] = dot(place[part], qf[...]).astype(jnp.bfloat16)
+            farsend[part] = dot(place[part], fout[...]).astype(jnp.bfloat16).reshape(
+                SHARDS, 16, 128
+            )
             return 0
 
         lax.fori_loop(0, SEGS, reorder, 0)
-        swap.wait()
-        far_flat = farsend.reshape(ROWS, 128)
-        lane = iota((SEG, 128), 1)
-        mine = lane // HEAD_DIM == half
-
-        def far(index, _):
-            rows = pl.ds(pl.multiple_of(index * SEG, SEG), SEG)
-            queries = qd[rows, :]
-            blocks = [(side, slice(at, at + SEG)) for side in range(2) for at in range(0, ROWS, SEG)]
-            upcoming = dot_t(queries, kv[0, 0, blocks[0][1], :])
-            peak = accum = None
-            for number, (side, keys) in enumerate(blocks):
-                scores = upcoming
-                if number + 1 < len(blocks):
-                    after, cut = blocks[number + 1]
-                    upcoming = dot_t(queries, kv[after, 0, cut, :])
-                top = jnp.max(scores, axis=-1, keepdims=True)
-                if number:
-                    top = jnp.maximum(peak, top)
-                    accum = accum * jnp.exp(peak - top)
-                term = dot(jnp.exp(scores - top).astype(jnp.bfloat16), kv[side, 1, keys, :])
-                accum = accum + term if number else term
-                peak = top
-            total = pltpu.roll(accum, 64, 1)
-            mixed = accum / total
-            level = peak + jnp.log(jnp.where(mine, 1.0, accum))
-            high = level.astype(jnp.bfloat16).astype(jnp.float32)
-            tail = jnp.where(lane % 64 < 32, high, level - high)
-            far_flat[rows, :] = jnp.where(mine, mixed, tail).astype(jnp.bfloat16)
-            return 0
-
-        lax.fori_loop(0, SEGS, far, 0)
 
         def give_far(step, _):
             to = peer(me, step)
@@ -304,28 +329,38 @@
         lax.fori_loop(1, SHARDS, give_far, 0)
         pltpu.make_async_copy(farsend.at[:, me], farrecv.at[me], frs).start()
 
-    lax.fori_loop(2, SEGS, deliver, 0)
-    wait_bytes(farrecv, frs)
-    load_c.wait()
+    def deliver_beside_far(part, _):
+        deliver(part, 0)
+
+        @pl.when(jnp.logical_and(head < HEADS, part < 2))
+        def _():
+            @pl.when(part == 0)
+            def _():
+                far_project(SEGS - 1)
+                swap(1).start()
+                swap(0).wait()
+                swap(1).wait()
+
+            lax.fori_loop(2 * part, 2 * part + 2, far, 0)
+            pl.when(part == 1)(return_far)
+
+        return 0
+
+    lax.fori_loop(0, SEGS - 1, deliver_beside_far, 0)
     load_o.wait()
     low = iota((SEG, 128), 1) < HEAD_DIM
     low_far = iota((16, 128), 1) < HEAD_DIM
 
-    def segment(part, _):
+    wait_bytes(send1.at[pl.ds(0, SHARDS - 1)], ssem1)
+    attn = send1.reshape(ROWS, WIDTH)
+    encst = recv1.reshape(ROWS, WIDTH)
+
+    def near_level(part):
+        slot = lax.rem(part, 2)
         wait_bytes(recv2.at[part], rsem2.at[part])
-        for src in range(SHARDS):
-            shift = RATE * (src % 2) + src // 2
-            rows = pl.ds(seg_base + shift, 16, stride=STRIDE)
-            for group in range(GROUPS):
-                xf[group, rows, :] = recv2[part, src, :, lanes(group)].astype(jnp.float32)
-
-        for at in range(0, SEG, 128):
-            normed[at : at + 128, :] = normalize(
-                jnp.concatenate(
-                    [xf[group, pl.ds(seg_base + at, 128), :] for group in range(GROUPS)], axis=1
-                ),
-                gain,
-            )
+        for at in range(0, SHARDS, 8):
+            rows = recv2[part, at : at + 8].reshape(128, WIDTH).astype(jnp.float32)
+            normed[16 * at : 16 * at + 128, :] = normalize(rows, gain)
 
         def project(index):
             for kind in range(3):
@@ -364,16 +399,17 @@
                 kept = []
                 total = pltpu.roll(jnp.where(low, accum1, accum0), 64, 1)
                 pair = number // 2
-                xf[pair, pl.ds(attn_base, SEG), :] = jnp.where(low, accum0, accum1) / total
-                lse[pair] = jnp.where(low, peak0, peak1) + jnp.log(total)
-
+                mix[slot, pair] = jnp.where(low, accum0, accum1) / total
+                lse[slot, pair] = jnp.where(low, peak0, peak1) + jnp.log(total)
+
+    def merge(part):
+        slot = lax.rem(part, 2)
         for src in range(FAR_OWNERS):
             number = src // 2
             pair, half = number // 2, number % 2
-            shift = RATE * (src % 2) + number
-            rows = pl.ds(attn_base + shift, 16, stride=STRIDE)
-            near_part = xf[pair, rows, :]
-            near_lse = lse[pair, pl.ds(shift, 16, stride=STRIDE), :]
+            rows = slice(16 * src, 16 * src + 16)
+            near_part = mix[slot, pair, rows, :]
+            near_lse = lse[slot, pair, rows, :]
             far_part = farrecv[src, part].astype(jnp.float32)
             other = HEAD_DIM * (1 - half)
             far_lse = far_part[:, other : other + 1] + far_part[:, other + 32 : other + 33]
@@ -382,45 +418,58 @@
             far_share = jnp.exp(far_lse - top)
             mixed = (near_share * near_part + far_share * far_part) / (near_share + far_share)
             mine = low_far if half == 0 else jnp.logical_not(low_far)
-            xf[pair, rows, :] = jnp.where(mine, mixed, near_part)
-
+            mix[slot, pair, rows, :] = jnp.where(mine, mixed, near_part)
+
+        here = pl.ds(pl.multiple_of(part * SEG, SEG), SEG)
         for group in range(GROUPS):
-            attn[:, lanes(group)] = xf[group, pl.ds(attn_base, SEG), :].astype(jnp.bfloat16)
-        seg_at = pl.multiple_of(part * SEG, SEG)
-
+            attn[here, lanes(group)] = mix[slot, group].astype(jnp.bfloat16)
         for index in range(3):
             cols = slice(index * 256, index * 256 + 256)
-            projected = dot(attn[...], wout[:, cols])
             term = lax.dot_general(
-                attn[...], xb[pl.ds(seg_at, SEG), cols], (((0,), (0,)), ((), ())),
+                attn[here, :], xb[here, cols], (((0,), (0,)), ((), ())),
                 preferred_element_type=jnp.float32,
             )
             for sub in range(2):
                 group = 2 * index + sub
-                encst[part, :, lanes(group)] = (
-                    xf[group, pl.ds(seg_base, SEG), :] + projected[:, lanes(sub)]
-                ).astype(jnp.bfloat16)
-                held = xf[group, pl.ds(grad_base, WIDTH), :]
                 piece = term[:, lanes(sub)]
-                xf[group, pl.ds(grad_base, WIDTH), :] = jnp.where(part == 0, piece, held + piece)
-
-        pltpu.make_async_copy(
-            encst.at[part], enc_hbm.at[pl.ds(seg_at, SEG)], esem.at[part]
-        ).start()
-        return 0
-
-    lax.fori_loop(0, SEGS, segment, 0)
+                grad[group] = jnp.where(part == 0, piece, grad[group] + piece)
+
+    def segment(step, _):
+        pl.when(step < SEGS)(functools.partial(near_level, step))
+
+        @pl.when(step == 0)
+        def _():
+            deliver(SEGS - 1, 0)
+
+        @pl.when(step == 1)
+        def _():
+            wait_bytes(farrecv, frs)
+
+        pl.when(step > 0)(functools.partial(merge, step - 1))
+        return 0
+
+    def finish(part, _):
+        here = pl.ds(pl.multiple_of(part * SEG, SEG), SEG)
+        inputs = recv2[part].reshape(SEG, WIDTH)
+        for index in range(3):
+            cols = slice(index * 256, index * 256 + 256)
+            projected = dot(attn[here, :], wout[:, cols])
+            summed = (inputs[:, cols].astype(jnp.float32) + projected).astype(jnp.bfloat16)
+            encst[here, cols] = dot(ordered[...], summed).astype(jnp.bfloat16)
+        pltpu.make_async_copy(encst.at[here], enc_hbm.at[here], esem.at[part]).start()
+        return 0
+
+    lax.fori_loop(0, SEGS + 1, segment, 0)
 
     for side in range(2):
         for group in range(3):
-            gsend[side, :, lanes(group)] = xf[
-                3 * side + group, pl.ds(grad_base, WIDTH), :
-            ].astype(jnp.bfloat16)
+            gsend[side, :, lanes(group)] = grad[3 * side + group].astype(jnp.bfloat16)
     join = pltpu.make_async_remote_copy(
         src_ref=gsend.at[1 - core], dst_ref=gmate, send_sem=jss, recv_sem=jrs,
         device_id={"seq": mate}, device_id_type=MESH,
     )
     join.start()
+    lax.fori_loop(0, 2, finish, 0)
     join.wait()
     both = gsend[core].astype(jnp.float32) + gmate[...].astype(jnp.float32)
     gpart[...] = both.astype(jnp.bfloat16).reshape(SHARDS // 2, 48, 384)
@@ -437,6 +486,7 @@
 
     lax.fori_loop(1, SHARDS // 2, give_grad, 0)
     pltpu.make_async_copy(gpart.at[head], grecv.at[head], grs).start()
+    lax.fori_loop(2, SEGS, finish, 0)
     wait_bytes(grecv, grs)
     ysend[...] = jnp.sum(grecv[...].astype(jnp.float32), axis=0).astype(jnp.bfloat16)
     for step in range(1, SLIDES):
@@ -460,10 +510,9 @@
     grad_ref[:, 384:] = fin[1]
 
     wait_bytes(dall.at[pl.ds(0, SHARDS - 1)], dssem)
-    wait_bytes(send1.at[pl.ds(0, SHARDS - 1)], ssem1)
     for part in range(SEGS):
         wait_bytes(send2.at[part, pl.ds(0, SHARDS - 1)], ssem2.at[part])
-        wait_bytes(encst.at[part], esem.at[part])
+        wait_bytes(encst.at[pl.ds(part * SEG, SEG)], esem.at[part])
 
     @pl.when(head < HEADS)
     def _():
@@ -474,8 +523,6 @@
 
 
 def body(tile_rows, block_dest, norm_gain, qkv_weight, out_weight, cotangent):
-    dests = jnp.pad(jnp.repeat(block_dest, 4, axis=1), ((0, 0), (0, 64)))
-    dests = jnp.broadcast_to(dests, (8, 128))
     bf16, f32 = jnp.bfloat16, jnp.float32
     dma = pltpu.SemaphoreType.DMA
     anywhere = pl.BlockSpec(memory_space=pl.ANY)
@@ -493,10 +540,13 @@
             pltpu.VMEM((GROUPS, ROWS, 128), f32),
             pltpu.VMEM((SHARDS, 64, WIDTH), bf16),
             pltpu.VMEM((SHARDS, 64, WIDTH), bf16),
+            pltpu.VMEM((8, 128), jnp.int32),
             pltpu.VMEM((SHARDS, 8, 128), jnp.int32),
             pltpu.VMEM((SEGS, SHARDS, 16, WIDTH), bf16),
             pltpu.VMEM((SEGS, SHARDS, 16, WIDTH), bf16),
             pltpu.VMEM((SEGS, SEG, ROWS), bf16),
+            pltpu.VMEM((SEG, SEG), bf16),
+            pltpu.VMEM((SEG, SEG), bf16),
             pltpu.VMEM((2, 2, ROWS, 128), bf16),
             pltpu.VMEM((ROWS, 128), bf16),
             pltpu.VMEM((ROWS, 128), bf16),
@@ -507,9 +557,9 @@
             pltpu.VMEM((WIDTH, WIDTH), bf16),
             pltpu.VMEM((SEG, WIDTH), bf16),
             pltpu.VMEM((SEG, 3 * WIDTH), bf16),
-            pltpu.VMEM((SEG, WIDTH), bf16),
-            pltpu.VMEM((PAIRS, SEG, 128), f32),
-            pltpu.VMEM((SEGS, SEG, WIDTH), bf16),
+            pltpu.VMEM((2, PAIRS, SEG, 128), f32),
+            pltpu.VMEM((2, PAIRS, SEG, 128), f32),
+            pltpu.VMEM((GROUPS, WIDTH, 128), f32),
             pltpu.VMEM((2, WIDTH, 384), bf16),
             pltpu.VMEM((WIDTH, 384), bf16),
             pltpu.VMEM((SHARDS // 2, 48, 384), bf16),
@@ -518,15 +568,16 @@
             pltpu.VMEM((SLIDES, 48, 384), bf16),
             pltpu.VMEM((2, 24, 384), f32),
             pltpu.VMEM((2, 24, 384), f32),
-            dma, dma((SEGS,)), dma, dma, dma((SEGS,)), dma((SEGS,)), dma, dma, dma, dma, dma, dma,
-            dma, dma, dma, dma, dma, dma, dma, dma, dma, dma, dma((SEGS,)),
+            dma, dma((SEGS,)), dma, dma, dma((SEGS,)), dma((SEGS,)), dma((2,)), dma((2,)),
+            dma, dma, dma, dma, dma, dma, dma, dma, dma, dma,
+            dma((SEGS,)), dma, dma, dma, dma((SEGS,)),
         ],
         compiler_params=pltpu.CompilerParams(
             collective_id=0, has_side_effects=True, vmem_limit_bytes=62 * 1024 * 1024
         ),
         name="slide_layer",
     )(
-        tile_rows.reshape(ROWS, WIDTH), dests, norm_gain.reshape(1, WIDTH),
+        tile_rows.reshape(ROWS, WIDTH), block_dest, norm_gain,
         qkv_weight, out_weight, cotangent.reshape(ROWS, WIDTH),
     )
     return encoded.reshape(1, ROWS, WIDTH), grad

time: 142 us -> 130 us (0.915)
  the two profiles are of different devices: /device:TPU:0 before, /device:TPU:19 now
where the time goes in v3:
time: 130 us; the launch traced here: 129 us
  Pallas kernels  124 us (95%)
  local copies, waits for them, and re-layouts  4.42 us (3%)
    pallas_call x1, Pallas kernels, body(): pl.pallas_call(kernel, out_shape=(jax.ShapeDtypeStruct((ROWS, WIDTH), bf1...  124 us
    unnamed x4, local copies, waits for them, and re-layouts  4.42 us

profile of v3, /device:TPU:19, one launch (start us, length us, event | category | flops | bytes accessed | tf_op | source)
XLA Modules:
  0.0 129.5 jit_solution(7374116966608666396)
XLA Ops:
  0.6 124.4 %slide_layer.1 = (bf16[2048,768]{1,0:T(8,128)(2,1)}, f32[24,768]{1,0:T(8,128)}) custom-call(bf16[2048,768]{1,0:T(8,128)(2,1)} %bitcast.4, s32[1,16]{1,0:T(1,128)} %dest_ref.1, f32[768]{0:T(1024)} %gain_ref.1, bf16[768,2304]{1,0:T(8,128)(2,1)} %wqkv_hbm.1, bf16[768,768]{1,0:T(8,128)(2,1)} %wout_hbm.1, bf16[2048,768]{1,0:T(8,128)(2,1)} %bitcast.5), custom_call_target="tpu_custom_call" | custom-call | tf_op jit(solution)/shard_map/slide_layer/pallas_call | solution.py:530
  125.1 0.0 copy-start
  125.1 3.8 %copy.10 = bf16[1,2048,768]{2,1,0:T(8,128)(2,1)} copy(bf16[1,2048,768]{2,1,0:T(8,128)(2,1)} %bitcast.3) | data formatting | bytes 6291456
  128.9 0.0 copy-done
  128.9 0.6 copy.11
Async XLA Ops:
  125.1 3.8 %copy-start = (f32[24,768]{1,0:T(8,128)S(1)}, f32[24,768]{1,0:T(8,128)}, u32[]{:S(2)}) copy-start(f32[24,768]{1,0:T(8,128)} %get-tuple-element.9) | copy-start | bytes 221188

commit v4 on v3

--- a/solution.py
+++ b/solution.py
@@ -99,10 +99,10 @@
 
 def kernel(
     x_hbm, dest_ref, gain_ref, wqkv_hbm, wout_hbm, cot_hbm, enc_hbm, grad_ref,
-    xb, xf, send1, recv1, dsend, dall, send2, recv2, place, ordered, classed, kv, qf, fout, farsend, farrecv,
-    wqkv, wfar, wout, normed, qkv, mix, lse, grad, gsend, gmate, gpart, grecv, ysend, yrecv, ysum, fin,
+    xb, send1, recv1, dsend, dall, send2, recv2, place, ordered, classed, kv, qf, fout, farsend, farrecv,
+    wqkv, wfar, wout, normed, qkv, mix, lse, grad, gsend, gmate, gpart, grecv, ysend, yrecv,
     ssem1, rsem1, dssem, drsem, ssem2, rsem2, kvs, kvr, fss, frs,
-    jss, jrs, gss, grs, yss, yrs, css, crs, xsem, wsem, osem, csem, esem,
+    jss, jrs, gss, grs, yss, yrs, xsem, wsem, osem, csem, esem,
 ):
     me = lax.axis_index("seq")
     dp = lax.axis_index("dp")
@@ -133,25 +133,44 @@
 
     lax.fori_loop(1, SHARDS, greet, 0)
     for step in range(1, SLIDES):
-        pl.semaphore_signal(
-            barrier, inc=1, device_id={"dp": lax.rem(dp + step, SLIDES)}, device_id_type=MESH
-        )
+        for across in range(2):
+            pl.semaphore_signal(
+                barrier, inc=1,
+                device_id={
+                    "dp": lax.rem(dp + step, SLIDES),
+                    "seq": me - core + lax.rem(core + across, 2),
+                },
+                device_id_type=MESH,
+            )
 
     spread = one_hot(iota((16, 128), 0) == iota((16, 128), 1) // 4)
     dests = dot(dest_ref[...].astype(jnp.float32).astype(jnp.bfloat16), spread)
     dsend[...] = jnp.broadcast_to(dests, (8, 128)).astype(jnp.int32)
 
-    def widen(index, _):
+    row, col = iota((SEG, SEG), 0), iota((SEG, SEG), 1)
+    classed[...] = one_hot(col == STRIDE * (row % 16) + row_class(row // 16))
+
+    def pack(index, _):
         wait_bytes(xb.at[pl.ds(0, SEG)], xsem.at[index])
         rows = pl.ds(pl.multiple_of(index * SEG, SEG), SEG)
-        for group in range(GROUPS):
-            xf[group, rows, :] = xb[rows, lanes(group)].astype(jnp.float32)
-        return 0
-
-    lax.fori_loop(0, SEGS, widen, 0)
+        found = dot(classed[...], xb[rows, :]).astype(jnp.bfloat16)
+        to_rows = pl.ds(pl.multiple_of(index * 16, 16), 16)
+        send1[:, to_rows, :] = found.reshape(SHARDS, 16, WIDTH)
+        return 0
+
+    lax.fori_loop(0, SEGS, pack, 0)
     load_c = pltpu.make_async_copy(cot_hbm, xb, csem)
     load_c.start()
-    pl.semaphore_wait(barrier, SHARDS - 1 + SLIDES - 1)
+    pl.semaphore_wait(barrier, SHARDS - 1 + 2 * (SLIDES - 1))
+
+    def scatter(step, _):
+        to = peer(me, step)
+        pltpu.make_async_remote_copy(
+            src_ref=send1.at[to], dst_ref=recv1.at[step], send_sem=ssem1,
+            recv_sem=rsem1.at[lax.div(step, 8)],
+            device_id={"seq": to}, device_id_type=MESH,
+        ).start()
+        return 0
 
     def tell(step, _):
         to = peer(me, step)
@@ -161,26 +180,10 @@
         ).start()
         return 0
 
+    lax.fori_loop(1, 8, scatter, 0)
     lax.fori_loop(1, SHARDS, tell, 0)
     pltpu.make_async_copy(dsend, dall.at[0], drsem).start()
-
-    def pack(to):
-        rows = pl.ds(row_class(to), 64, stride=STRIDE)
-        for group in range(GROUPS):
-            send1[to, :, lanes(group)] = xf[group, rows, :].astype(jnp.bfloat16)
-
-    def scatter(step, _):
-        to = peer(me, step)
-        pack(to)
-        pltpu.make_async_remote_copy(
-            src_ref=send1.at[to], dst_ref=recv1.at[step], send_sem=ssem1,
-            recv_sem=rsem1.at[lax.div(step, 8)],
-            device_id={"seq": to}, device_id_type=MESH,
-        ).start()
-        return 0
-
-    lax.fori_loop(1, SHARDS, scatter, 0)
-    pack(me)
+    lax.fori_loop(8, SHARDS, scatter, 0)
     pltpu.make_async_copy(send1.at[me], recv1.at[0], rsem1.at[0]).start()
 
     wait_bytes(dall, drsem)
@@ -192,9 +195,7 @@
         return 0
 
     lax.fori_loop(0, SEGS, build, 0)
-    row, col = iota((SEG, SEG), 0), iota((SEG, SEG), 1)
     ordered[...] = one_hot(col == 32 * (row % RATE) + 16 * (row % STRIDE // RATE) + row // STRIDE)
-    classed[...] = one_hot(col == STRIDE * (row % 16) + row_class(row // 16))
     load_c.wait()
 
     def class_order(part, _):
@@ -261,17 +262,15 @@
 
     def moved(part, group):
         rows = slice(group * SEG, group * SEG + SEG)
-        return dot(place[part, :, rows], gathered[rows, :])
+        found = dot(place[part, :, rows], gathered[rows, :]).astype(jnp.bfloat16)
+        return found.reshape(SHARDS, 16, WIDTH)
 
     for group in range(SEGS - 1):
         wait_bytes(recv1.at[pl.ds(8 * group, 8)], rsem1.at[group])
 
         def regroup(part, _, group=group):
             term = moved(part, group)
-            at = pl.ds(pl.multiple_of(part * SEG, SEG), SEG)
-            for cols in range(GROUPS):
-                piece = term[:, lanes(cols)]
-                xf[cols, at, :] = piece if group == 0 else xf[cols, at, :] + piece
+            send2[part] = term if group == 0 else send2[part] + term
             return 0
 
         @pl.when(head < HEADS)
@@ -283,11 +282,7 @@
         lax.fori_loop(0, SEGS, regroup, 0)
 
     def deliver(part, _):
-        term = moved(part, SEGS - 1)
-        at = pl.ds(pl.multiple_of(part * SEG, SEG), SEG)
-        for cols in range(GROUPS):
-            piece = (xf[cols, at, :] + term[:, lanes(cols)]).astype(jnp.bfloat16)
-            send2[part, :, :, lanes(cols)] = piece.reshape(SHARDS, 16, 128)
+        send2[part] = send2[part] + moved(part, SEGS - 1)
 
         def give(step, _):
             to = peer(me, step)
@@ -332,21 +327,24 @@
     def deliver_beside_far(part, _):
         deliver(part, 0)
 
-        @pl.when(jnp.logical_and(head < HEADS, part < 2))
+        @pl.when(jnp.logical_and(head < HEADS, part == 0))
         def _():
-            @pl.when(part == 0)
+            far_project(SEGS - 1)
+            swap(1).start()
+
+        @pl.when(jnp.logical_and(head < HEADS, jnp.logical_or(part == 1, part == 2)))
+        def _():
+            @pl.when(part == 1)
             def _():
-                far_project(SEGS - 1)
-                swap(1).start()
                 swap(0).wait()
                 swap(1).wait()
 
-            lax.fori_loop(2 * part, 2 * part + 2, far, 0)
-            pl.when(part == 1)(return_far)
-
-        return 0
-
-    lax.fori_loop(0, SEGS - 1, deliver_beside_far, 0)
+            lax.fori_loop(2 * part - 2, 2 * part, far, 0)
+            pl.when(part == 2)(return_far)
+
+        return 0
+
+    lax.fori_loop(0, SEGS, deliver_beside_far, 0)
     load_o.wait()
     low = iota((SEG, 128), 1) < HEAD_DIM
     low_far = iota((16, 128), 1) < HEAD_DIM
@@ -437,10 +435,6 @@
     def segment(step, _):
         pl.when(step < SEGS)(functools.partial(near_level, step))
 
-        @pl.when(step == 0)
-        def _():
-            deliver(SEGS - 1, 0)
-
         @pl.when(step == 1)
         def _():
             wait_bytes(farrecv, frs)
@@ -461,15 +455,18 @@
 
     lax.fori_loop(0, SEGS + 1, segment, 0)
 
-    for side in range(2):
+    def cast_grad(side):
         for group in range(3):
             gsend[side, :, lanes(group)] = grad[3 * side + group].astype(jnp.bfloat16)
+
+    cast_grad(1 - core)
     join = pltpu.make_async_remote_copy(
         src_ref=gsend.at[1 - core], dst_ref=gmate, send_sem=jss, recv_sem=jrs,
         device_id={"seq": mate}, device_id_type=MESH,
     )
     join.start()
-    lax.fori_loop(0, 2, finish, 0)
+    cast_grad(core)
+    finish(0, 0)
     join.wait()
     both = gsend[core].astype(jnp.float32) + gmate[...].astype(jnp.float32)
     gpart[...] = both.astype(jnp.bfloat16).reshape(SHARDS // 2, 48, 384)
@@ -486,28 +483,27 @@
 
     lax.fori_loop(1, SHARDS // 2, give_grad, 0)
     pltpu.make_async_copy(gpart.at[head], grecv.at[head], grs).start()
-    lax.fori_loop(2, SEGS, finish, 0)
+    lax.fori_loop(1, SEGS, finish, 0)
     wait_bytes(grecv, grs)
-    ysend[...] = jnp.sum(grecv[...].astype(jnp.float32), axis=0).astype(jnp.bfloat16)
-    for step in range(1, SLIDES):
-        pltpu.make_async_remote_copy(
-            src_ref=ysend, dst_ref=yrecv.at[dp], send_sem=yss, recv_sem=yrs,
-            device_id={"dp": lax.rem(dp + step, SLIDES)}, device_id_type=MESH,
-        ).start()
-    pltpu.make_async_copy(ysend, yrecv.at[dp], yrs).start()
+    summed = jnp.sum(grecv[...].astype(jnp.float32), axis=0)
+    ysend[0] = summed[:24]
+    ysend[1] = summed[24:]
+    for step in range(SLIDES):
+        for across in range(2):
+            side = lax.rem(core + across, 2)
+            landing = yrecv.at[core, dp]
+            if step or across:
+                pltpu.make_async_remote_copy(
+                    src_ref=ysend.at[side], dst_ref=landing, send_sem=yss, recv_sem=yrs,
+                    device_id={"dp": lax.rem(dp + step, SLIDES), "seq": me - core + side},
+                    device_id_type=MESH,
+                ).start()
+            else:
+                pltpu.make_async_copy(ysend.at[side], landing, yrs).start()
     wait_bytes(yrecv, yrs)
-    whole = jnp.sum(yrecv[...].astype(jnp.float32), axis=0)
-    ysum[0] = whole[:24]
-    ysum[1] = whole[24:]
-    last = pltpu.make_async_remote_copy(
-        src_ref=ysum.at[1 - core], dst_ref=fin.at[core], send_sem=css, recv_sem=crs,
-        device_id={"seq": mate}, device_id_type=MESH,
-    )
-    last.start()
-    fin[core] = ysum[core]
-    last.wait()
-    grad_ref[:, :384] = fin[0]
-    grad_ref[:, 384:] = fin[1]
+    for side in range(2):
+        total = (yrecv[side, 0] + yrecv[side, 1]) + (yrecv[side, 2] + yrecv[side, 3])
+        grad_ref[:, 384 * side : 384 * side + 384] = total
 
     wait_bytes(dall.at[pl.ds(0, SHARDS - 1)], dssem)
     for part in range(SEGS):
@@ -519,7 +515,27 @@
         wait_bytes(farsend.at[:, pl.ds(0, SHARDS - 1)], fss)
 
     wait_bytes(gpart.at[pl.ds(0, SHARDS // 2 - 1)], gss)
-    wait_bytes(yrecv.at[pl.ds(0, SLIDES - 1)], yss)
+    wait_bytes(yrecv.at[0], yss)
+    wait_bytes(yrecv.at[1, pl.ds(0, SLIDES - 1)], yss)
+
+
+def hand_on(src, dst, held, in_sems, out_sems):
+    pieces = [pl.ds(at, SEG) for at in range(0, ROWS, SEG)]
+    into = [
+        pltpu.make_async_copy(src.at[rows], held.at[rows], in_sems.at[number])
+        for number, rows in enumerate(pieces)
+    ]
+    out = [
+        pltpu.make_async_copy(held.at[rows], dst.at[rows], out_sems.at[number])
+        for number, rows in enumerate(pieces)
+    ]
+    for copy in into:
+        copy.start()
+    for first, second in zip(into, out):
+        first.wait()
+        second.start()
+    for copy in out:
+        copy.wait()
 
 
 def body(tile_rows, block_dest, norm_gain, qkv_weight, out_weight, cotangent):
@@ -537,7 +553,6 @@
         out_specs=(anywhere, vmem),
         scratch_shapes=[
             pltpu.VMEM((ROWS, WIDTH), bf16),
-            pltpu.VMEM((GROUPS, ROWS, 128), f32),
             pltpu.VMEM((SHARDS, 64, WIDTH), bf16),
             pltpu.VMEM((SHARDS, 64, WIDTH), bf16),
             pltpu.VMEM((8, 128), jnp.int32),
@@ -564,12 +579,10 @@
             pltpu.VMEM((WIDTH, 384), bf16),
             pltpu.VMEM((SHARDS // 2, 48, 384), bf16),
             pltpu.VMEM((SHARDS // 2, 48, 384), bf16),
-            pltpu.VMEM((48, 384), bf16),
-            pltpu.VMEM((SLIDES, 48, 384), bf16),
             pltpu.VMEM((2, 24, 384), f32),
-            pltpu.VMEM((2, 24, 384), f32),
+            pltpu.VMEM((2, SLIDES, 24, 384), f32),
             dma, dma((SEGS,)), dma, dma, dma((SEGS,)), dma((SEGS,)), dma((2,)), dma((2,)),
-            dma, dma, dma, dma, dma, dma, dma, dma, dma, dma,
+            dma, dma, dma, dma, dma, dma, dma, dma,
             dma((SEGS,)), dma, dma, dma, dma((SEGS,)),
         ],
         compiler_params=pltpu.CompilerParams(
@@ -580,6 +593,14 @@
         tile_rows.reshape(ROWS, WIDTH), block_dest, norm_gain,
         qkv_weight, out_weight, cotangent.reshape(ROWS, WIDTH),
     )
+    encoded = pl.pallas_call(
+        hand_on,
+        out_shape=jax.ShapeDtypeStruct((ROWS, WIDTH), bf16),
+        in_specs=[anywhere],
+        out_specs=anywhere,
+        scratch_shapes=[pltpu.VMEM((ROWS, WIDTH), bf16), dma((SEGS,)), dma((SEGS,))],
+        name="hand_on",
+    )(encoded)
     return encoded.reshape(1, ROWS, WIDTH), grad
 
 

time: 130 us -> 127 us (0.977)
  the two profiles are of different devices: /device:TPU:19 before, /device:TPU:0 now
where the time goes in v4:
time: 127 us; the launch traced here: 126 us
  Pallas kernels  125 us (98%)
    pallas_call x1, Pallas kernels, body(): pl.pallas_call(kernel, out_shape=(jax.ShapeDtypeStruct((ROWS, WIDTH), bf1...  122 us
    pallas_call x1, Pallas kernels, body(): pl.pallas_call(hand_on, out_shape=jax.ShapeDtypeStruct((ROWS, WIDTH), bf1...  2.89 us

profile of v4, /device:TPU:0, one launch (start us, length us, event | category | flops | bytes accessed | tf_op | source)
XLA Modules:
  0.0 126.0 jit_solution(324649029283537338)
XLA Ops:
  0.6 121.8 %slide_layer.1 = (bf16[2048,768]{1,0:T(8,128)(2,1)}, f32[24,768]{1,0:T(8,128)}) custom-call(bf16[2048,768]{1,0:T(8,128)(2,1)} %bitcast.4, s32[1,16]{1,0:T(1,128)} %dest_ref.1, f32[768]{0:T(1024)} %gain_ref.1, bf16[768,2304]{1,0:T(8,128)(2,1)} %wqkv_hbm.1, bf16[768,768]{1,0:T(8,128)(2,1)} %wout_hbm.1, bf16[2048,768]{1,0:T(8,128)(2,1)} %bitcast.5), custom_call_target="tpu_custom_call" | custom-call | tf_op jit(solution)/shard_map/slide_layer/pallas_call | solution.py:546
  122.4 0.0 copy-start
  122.4 2.9 %hand_on.1 = bf16[2048,768]{1,0:T(8,128)(2,1)} custom-call(bf16[2048,768]{1,0:T(8,128)(2,1)} %get-tuple-element.4.src), custom_call_target="tpu_custom_call" | custom-call | tf_op jit(solution)/shard_map/hand_on/pallas_call | solution.py:596
  125.3 0.0 copy-done
  125.3 0.6 copy.9
Async XLA Ops:
  122.4 2.9 %copy-start = (f32[24,768]{1,0:T(8,128)S(1)}, f32[24,768]{1,0:T(8,128)}, u32[]{:S(2)}) copy-start(f32[24,768]{1,0:T(8,128)} %get-tuple-element.9) | copy-start | bytes 221188

commit v5 on v4

--- a/solution.py
+++ b/solution.py
@@ -38,16 +38,16 @@
 def peer(me, step):
     z, x, c = lax.div(me, 8), lax.rem(lax.div(me, 2), 4), lax.rem(me, 2)
     dz = lax.rem(step, 4)
-    dx = lax.rem(step + lax.div(step, 8), 4)
-    dc = lax.rem(lax.div(step, 4), 2)
+    dx = lax.rem(step + lax.rem(lax.div(step, 4), 4), 4)
+    dc = lax.div(step, 16)
     return lax.rem(z + dz, 4) * 8 + lax.rem(x + dx, 4) * 2 + lax.rem(c + dc, 2)
 
 
 def origin(me, step):
     z, x, c = lax.div(me, 8), lax.rem(lax.div(me, 2), 4), lax.rem(me, 2)
     dz = lax.rem(step, 4)
-    dx = lax.rem(step + lax.div(step, 8), 4)
-    dc = lax.rem(lax.div(step, 4), 2)
+    dx = lax.rem(step + lax.rem(lax.div(step, 4), 4), 4)
+    dc = lax.div(step, 16)
     return lax.rem(z + 4 - dz, 4) * 8 + lax.rem(x + 4 - dx, 4) * 2 + lax.rem(c + 2 - dc, 2)
 
 

time: 127 us -> 127 us (level)
  no operation moved by 1% of the time
where the time goes in v5:
time: 127 us; the launch traced here: 125 us
  Pallas kernels  124 us (98%)
    pallas_call x1, Pallas kernels, body(): pl.pallas_call(kernel, out_shape=(jax.ShapeDtypeStruct((ROWS, WIDTH), bf1...  121 us
    pallas_call x1, Pallas kernels, body(): pl.pallas_call(hand_on, out_shape=jax.ShapeDtypeStruct((ROWS, WIDTH), bf1...  2.89 us

profile of v5, /device:TPU:0, one launch (start us, length us, event | category | flops | bytes accessed | tf_op | source)
XLA Modules:
  0.0 125.4 jit_solution(12797592234570106575)
XLA Ops:
  0.6 121.3 %slide_layer.1 = (bf16[2048,768]{1,0:T(8,128)(2,1)}, f32[24,768]{1,0:T(8,128)}) custom-call(bf16[2048,768]{1,0:T(8,128)(2,1)} %bitcast.4, s32[1,16]{1,0:T(1,128)} %dest_ref.1, f32[768]{0:T(1024)} %gain_ref.1, bf16[768,2304]{1,0:T(8,128)(2,1)} %wqkv_hbm.1, bf16[768,768]{1,0:T(8,128)(2,1)} %wout_hbm.1, bf16[2048,768]{1,0:T(8,128)(2,1)} %bitcast.5), custom_call_target="tpu_custom_call" | custom-call | tf_op jit(solution)/shard_map/slide_layer/pallas_call | solution.py:546
  121.9 0.0 copy-start
  121.9 2.9 %hand_on.1 = bf16[2048,768]{1,0:T(8,128)(2,1)} custom-call(bf16[2048,768]{1,0:T(8,128)(2,1)} %get-tuple-element.4.src), custom_call_target="tpu_custom_call" | custom-call | tf_op jit(solution)/shard_map/hand_on/pallas_call | solution.py:596
  124.8 0.0 copy-done
  124.8 0.6 copy.9
Async XLA Ops:
  121.9 2.9 %copy-start = (f32[24,768]{1,0:T(8,128)S(1)}, f32[24,768]{1,0:T(8,128)}, u32[]{:S(2)}) copy-start(f32[24,768]{1,0:T(8,128)} %get-tuple-element.9) | copy-start | bytes 221188
